TPU v7x, 1024 devices: a whole 4x4x32 slice. The times are simulated.
1024 devices in a mesh: dp: 128 (over z, x), tm: 8 (over y, core).
Axes of the slice: x: 4, y: 4, z: 32, core: 2. Of those that a mesh axis runs over, the one named last changes fastest.
Arguments:
- frames: bfloat16 [4096, 96, 1024], P(('dp', 'tm')), may hold values from -6 to 6
- texts: bfloat16 [8192, 1024], P(('dp', 'tm')), may hold values from -6 to 6
- w_query: bfloat16 [1024, 1024], replicated, may hold values from -0.1875 to 0.1875
- w_key: bfloat16 [1024, 1024], replicated, may hold values from -0.1875 to 0.1875
- w_value: bfloat16 [1024, 1024], replicated, may hold values from -0.1875 to 0.1875
- w_out: bfloat16 [1024, 1024], replicated, may hold values from -0.1875 to 0.1875
- frame_counts: int32 [4096], P(('dp', 'tm')), may hold values from 1 to 96, as said below
- clip_pos: int32 [4096], P(('dp', 'tm')), may hold values from 0 to 191
Outputs:
- similar: float32 [4096, 3, 64], P(('dp', 'tm'))
- clip_loss: float32 [4096], P(('dp', 'tm'))
- text_lse: float32 [8192], P(('dp', 'tm'))
Inputs may be any that keep to these rules, and one draw needn't show every extreme that they name: `frame_counts`: some clip has all 96 frames valid and some clip only one.
All inputs are finite; a program needn't handle non-finite values.
Results may differ from a plain program's by a relative error of at most 0.0061.
Values may be sent and summed in bfloat16 or wider, within the bound.
No kernel may reach another device: no remote copies, remote signals or barrier semaphores. Data moves between devices by JAX's collectives and lax.ppermute only.
A program may use at most 32 MiB of HBM per device.

v0:
```python
import math

import jax
import jax.numpy as jnp
from jax import lax
from jax.sharding import PartitionSpec as P

HOPS = 2


LOGIT_SCALE = 32.0
EPSILON = 1e-06


def passed_along(value, axis, steps):
    count = lax.axis_size(axis)
    pairs = [(source, (source + steps) % count) for source in range(count)]
    return lax.ppermute(value, axis, pairs)


def cosine_scaled(pooled, text_rows):
    inner = jnp.sum(pooled * text_rows, axis=-1)
    pooled_sq = jnp.sum(pooled * pooled, axis=-1)
    text_sq = jnp.sum(text_rows * text_rows, axis=-1)
    return LOGIT_SCALE * inner / jnp.sqrt((pooled_sq + EPSILON) * (text_sq + EPSILON))


def local(frames, texts, w_query, w_key, w_value, w_out, frame_counts, clip_pos):
    clip_rows, frame_total, feature_width = frames.shape
    slice_rows = texts.shape[0]
    tm_count = lax.axis_size("tm")
    block_rows = slice_rows * tm_count
    band_rows_total = (HOPS + 1) * block_rows
    frame_flat = frames.reshape(-1, feature_width)
    key_rows = (
        jnp.dot(frame_flat, w_key, preferred_element_type=jnp.float32)
        .astype(jnp.bfloat16)
        .reshape(clip_rows, frame_total, feature_width)
    )
    value_rows = (
        jnp.dot(frame_flat, w_value, preferred_element_type=jnp.float32)
        .astype(jnp.bfloat16)
        .reshape(clip_rows, frame_total, feature_width)
    )
    pieces = [texts]
    current = texts
    for step in range(1, HOPS + 1):
        current = passed_along(current, "dp", 1)
        pieces.append(current)
    band_slice = jnp.stack(pieces, axis=0)
    band_text = lax.all_gather(band_slice, "tm", axis=1, tiled=True).reshape(
        band_rows_total, feature_width
    )
    band_query = jnp.dot(band_text, w_query, preferred_element_type=jnp.float32).astype(
        jnp.bfloat16
    )
    frame_index = jnp.arange(frame_total, dtype=jnp.int32)
    valid_mask = frame_index[None, None, :] < frame_counts[:, None, None]
    scores = jnp.einsum(
        "tk,cfk->ctf", band_query, key_rows, preferred_element_type=jnp.float32
    ) / math.sqrt(feature_width)
    frame_weights = jnp.where(valid_mask, jnp.exp(scores), 0.0)
    weight_sum = jnp.sum(frame_weights, axis=-1)
    weighted = jnp.einsum(
        "ctf,cfk->ctk",
        frame_weights.astype(jnp.bfloat16),
        value_rows,
        preferred_element_type=jnp.float32,
    )
    attended = (weighted / weight_sum[..., None]).astype(jnp.bfloat16)
    pooled = jnp.dot(
        attended.reshape(-1, feature_width), w_out, preferred_element_type=jnp.float32
    ).reshape(clip_rows, band_rows_total, feature_width)
    similar = cosine_scaled(pooled, band_text.astype(jnp.float32)[None])
    exp_sims = jnp.exp(similar)
    band_index = jnp.arange(band_rows_total, dtype=jnp.int32)
    hit_mask = band_index[None, :] == clip_pos[:, None]
    picked = jnp.sum(jnp.where(hit_mask, similar, 0.0), axis=-1)
    clip_loss = jnp.log(jnp.sum(exp_sims, axis=-1)) - picked
    term_rows = jnp.sum(exp_sims, axis=0).reshape(HOPS + 1, block_rows)
    shares = lax.psum_scatter(term_rows, "tm", scatter_dimension=1, tiled=True)
    back_sums = shares[HOPS]
    for step in range(HOPS - 1, -1, -1):
        back_sums = passed_along(back_sums, "dp", -1) + shares[step]
    text_lse = jnp.log(back_sums)
    similar_out = similar.reshape(clip_rows, HOPS + 1, block_rows)
    return (similar_out, clip_loss, text_lse)


def solution(mesh):
    in_specs = (
        P(("dp", "tm"), None, None),
        P(("dp", "tm"), None),
        P(),
        P(),
        P(),
        P(),
        P(("dp", "tm")),
        P(("dp", "tm")),
    )
    out_specs = (P(("dp", "tm"), None, None), P(("dp", "tm")), P(("dp", "tm")))
    return jax.shard_map(local, mesh=mesh, in_specs=in_specs, out_specs=out_specs, check_vma=False)
```

profile of v0, /device:TPU:8, one launch (start us, length us, event | category | flops | bytes accessed | tf_op | source)
XLA Modules:
  0.0 78.5 jit_solution(8160833878351441858)
XLA Ops:
  0.6 0.0 copy-start
  0.6 3.5 %collective-permute-start = (bf16[8,1024]{1,0:T(8,128)(2,1)}, bf16[8,1024]{1,0:T(8,128)(2,1)S(1)}, u32[]{:S(2)}, u32[]{:S(2)}) collective-permute-start(bf16[8,1024]{1,0:T(8,128)(2,1)} %param.9), channel_id=1, source_target_pairs={{0,8},{8,16},{16,24},{24,32},{32,40},{40,48},{48,56},{56,64},{64,7... | collective-permute-start | bytes 49160 | tf_op jit(solution)/shard_map/ppermute | solution.py:18
  4.2 0.0 copy-done
  4.2 0.0 copy-start.3
  4.2 0.0 copy-start.4
  4.2 3.2 %convolution_convert_fusion.1 = bf16[384,1024]{1,0:T(8,128)(2,1)} fusion(bf16[384,1024]{1,0:T(8,128)(2,1)} %bitcast.45, bf16[1024,1024]{1,0:T(8,128)(2,1)S(1)} %copy-done), kind=kOutput, calls=%fused_computation.6 | convolution fusion | flops 805699584 | bytes 3670016 | tf_op jit(solution)/shard_map/dot_general | solution.py:36
  7.4 0.0 copy-done.3
  7.4 0.0 copy-done.4
  7.4 0.0 copy-start.5
  7.4 0.0 copy-start.1
  7.4 1.9 %convolution_convert_fusion = bf16[384,1024]{1,0:T(8,128)(2,1)} fusion(bf16[384,1024]{1,0:T(8,128)(2,1)S(1)} %bitcast.46, bf16[1024,1024]{1,0:T(8,128)(2,1)S(1)} %copy-done.3), kind=kOutput, calls=%fused_computation.5 | convolution fusion | flops 805699584 | bytes 3670016 | tf_op jit(solution)/shard_map/dot_general | solution.py:41
  9.3 14.3 %collective-permute-done = bf16[8,1024]{1,0:T(8,128)(2,1)S(1)} collective-permute-done((bf16[8,1024]{1,0:T(8,128)(2,1)}, bf16[8,1024]{1,0:T(8,128)(2,1)S(1)}, u32[]{:S(2)}, u32[]{:S(2)}) %collective-permute-start) | collective-permute-done | bytes 16416 | tf_op jit(solution)/shard_map/ppermute | solution.py:18
  23.6 1.9 %collective-permute-start.1 = (bf16[8,1024]{1,0:T(8,128)(2,1)S(1)}, bf16[8,1024]{1,0:T(8,128)(2,1)S(1)}, u32[]{:S(2)}, u32[]{:S(2)}) collective-permute-start(bf16[8,1024]{1,0:T(8,128)(2,1)S(1)} %collective-permute-done), channel_id=1, source_target_pairs={{0,8},{8,16},{16,24},{24,32},{32,40},{40,48},{48,56},{56,64},{64,7... | collective-permute-start | bytes 49160 | tf_op jit(solution)/shard_map/ppermute | solution.py:18
  25.5 0.0 copy-done.5
  25.5 0.1 iota_compare_fusion.1
  25.6 1.3 %dynamic-slice = u32[1]{0:T(128)} dynamic-slice(u32[1024]{0:T(1024)} %constant.16, u32[]{:T(128)S(6)} %add.42), dynamic_slice_sizes={1} | dynamic-slice | bytes 12
  27.5 5.0 %collective-permute-done.1 = bf16[8,1024]{1,0:T(8,128)(2,1)S(1)} collective-permute-done((bf16[8,1024]{1,0:T(8,128)(2,1)S(1)}, bf16[8,1024]{1,0:T(8,128)(2,1)S(1)}, u32[]{:S(2)}, u32[]{:S(2)}) %collective-permute-start.1) | collective-permute-done | bytes 16416 | tf_op jit(solution)/shard_map/ppermute | solution.py:18
  32.5 0.0 copy-done.1
  32.5 13.2 %all_gather.3 = bf16[3,64,1024]{2,1,0:T(8,128)(2,1)S(1)} all-gather(bf16[3,8,1024]{2,1,0:T(8,128)(2,1)S(1)} %pad_maximum_fusion), channel_id=1, replica_groups=mesh['dp'=128,'tm'=8] {'tm'}, dimensions={1}, use_global_device_ids=true | all-gather | bytes 442368 | tf_op jit(solution)/shard_map/all_gather | solution.py:51
  45.7 0.2 multiply_reduce_fusion.2
  45.9 0.1 convert_element_type.31
  46.0 0.1 add.38
  46.1 2.8 %fusion.9 = (f32[4,192]{1,0:T(4,128)S(1)}, bf16[4,192,96]{1,2,0:T(8,128)(2,1)S(1)}) fusion(bf16[4,96,1024]{2,1,0:T(8,128)(2,1)} %bitcast.48, bf16[192,1024]{1,0:T(8,128)(2,1)S(1)} %bitcast.41, bf16[1024,1024]{1,0:T(8,128)(2,1)} %param.10, pred[4,96]{1,0:T(4,128)(4,1)S(1)} %iota_compare_fusion.1), kind=kOutput, calls=%fused_computation.32 | convolution fusion | flops 554138880 | bytes 3427712 | tf_op jit(solution)/shard_map/tk,cfk->ctf/dot_general | solution.py:59
  48.9 0.0 copy-start.2
  48.9 4.3 %multiply_reduce_fusion = (f32[4,192]{1,0:T(4,128)S(1)}, f32[4,192]{1,0:T(4,128)S(1)}) fusion(f32[192,1024]{1,0:T(8,128)S(1)} %convert_element_type.31, bf16[1024,1024]{1,0:T(8,128)(2,1)} %param.13, bf16[4,96,1024]{2,1,0:T(8,128)(2,1)} %bitcast.47, f32[4,192]{1,0:T(4,128)S(1)} %get-tuple-element.17, bf16[4,192,96]{1,2,0:T(8,128)(2,1)S(1)} %get-tuple-element.18), kind=kOutput, calls=%fused_computation | convolution fusion | flops 1766324736 | bytes 3826688 | tf_op jit(solution)/shard_map/dot_general | solution.py:71
  53.2 0.0 copy-done.2
  53.2 0.2 exponential_reduce_fusion
  53.4 0.1 reshape.80
  53.5 12.1 %all-reduce = f32[3,64]{1,0:T(4,128)S(1)} all-reduce(f32[3,64]{1,0:T(4,128)S(1)} %reshape.80), channel_id=2, replica_groups=mesh['dp'=128,'tm'=8] {'tm'}, use_global_device_ids=true, to_apply=%region_7.8.clone | all-reduce | flops 192 | bytes 1536
  65.6 0.1 constant_dynamic-slice_fusion
  65.7 2.2 %collective-permute-start.2 = (f32[8]{0:T(128)S(1)}, f32[8]{0:T(128)S(1)}, u32[]{:S(2)}, u32[]{:S(2)}) collective-permute-start(f32[8]{0:T(128)S(1)} %slice_bitcast_fusion), channel_id=1, source_target_pairs={{0,1016},{8,0},{16,8},{24,16},{32,24},{40,32},{48,40},{56,48},{64,... | collective-permute-start | bytes 104 | tf_op jit(solution)/shard_map/ppermute | solution.py:18
  67.9 0.1 add.35
  68.0 0.1 mul.44
  68.1 0.6 copy.13
  68.7 0.5 log_subtract_fusion
  69.2 1.9 %collective-permute-done.2 = f32[8]{0:T(128)S(1)} collective-permute-done((f32[8]{0:T(128)S(1)}, f32[8]{0:T(128)S(1)}, u32[]{:S(2)}, u32[]{:S(2)}) %collective-permute-start.2) | collective-permute-done | bytes 64 | tf_op jit(solution)/shard_map/ppermute | solution.py:18
  71.1 5.6 %collective-permute-start.3 = (f32[8]{0:T(128)S(1)}, f32[8]{0:T(128)S(1)}, u32[]{:S(2)}, u32[]{:S(2)}) collective-permute-start(f32[8]{0:T(128)S(1)} %bitcast_add_fusion.1), channel_id=1, source_target_pairs={{0,1016},{8,0},{16,8},{24,16},{32,24},{40,32},{48,40},{56,48},{64,... | collective-permute-start | bytes 104 | tf_op jit(solution)/shard_map/ppermute | solution.py:18
  76.7 1.3 %collective-permute-done.3 = f32[8]{0:T(128)S(1)} collective-permute-done((f32[8]{0:T(128)S(1)}, f32[8]{0:T(128)S(1)}, u32[]{:S(2)}, u32[]{:S(2)}) %collective-permute-start.3) | collective-permute-done | bytes 64 | tf_op jit(solution)/shard_map/ppermute | solution.py:18
  77.9 0.5 fusion.8
  (6 shorter events, 0.0 us)
Async XLA Ops:
  0.6 3.6 %copy-start = (bf16[1024,1024]{1,0:T(8,128)(2,1)S(1)}, bf16[1024,1024]{1,0:T(8,128)(2,1)}, u32[]{:S(2)}) copy-start(bf16[1024,1024]{1,0:T(8,128)(2,1)} %param.11) | copy-start | bytes 6291460
  0.6 22.9 %collective-permute-start = (bf16[8,1024]{1,0:T(8,128)(2,1)}, bf16[8,1024]{1,0:T(8,128)(2,1)S(1)}, u32[]{:S(2)}, u32[]{:S(2)}) collective-permute-start(bf16[8,1024]{1,0:T(8,128)(2,1)} %param.9), channel_id=1, source_target_pairs={{0,8},{8,16},{16,24},{24,32},{32,40},{40,48},{48,56},{56,64},{64,7... | collective-permute-start | bytes 49160 | tf_op jit(solution)/shard_map/ppermute | solution.py:18
  4.2 3.2 %copy-start.3 = (bf16[1024,1024]{1,0:T(8,128)(2,1)S(1)}, bf16[1024,1024]{1,0:T(8,128)(2,1)}, u32[]{:S(2)}) copy-start(bf16[1024,1024]{1,0:T(8,128)(2,1)} %param.12) | copy-start | bytes 6291460
  4.2 3.2 %copy-start.4 = (bf16[4,96,1024]{2,1,0:T(8,128)(2,1)S(1)}, bf16[4,96,1024]{2,1,0:T(8,128)(2,1)}, u32[]{:S(2)}) copy-start(bf16[4,96,1024]{2,1,0:T(8,128)(2,1)} %param.8) | copy-start | bytes 2359300
  7.4 18.1 %copy-start.5 = (s32[4]{0:T(128)S(1)}, s32[4]{0:T(128)}, u32[]{:S(2)}) copy-start(s32[4]{0:T(128)} %param.14) | copy-start | bytes 52
  7.4 25.1 %copy-start.1 = (bf16[8,1024]{1,0:T(8,128)(2,1)S(1)}, bf16[8,1024]{1,0:T(8,128)(2,1)}, u32[]{:S(2)}) copy-start(bf16[8,1024]{1,0:T(8,128)(2,1)} %param.9) | copy-start | bytes 49156
  23.6 8.9 %collective-permute-start.1 = (bf16[8,1024]{1,0:T(8,128)(2,1)S(1)}, bf16[8,1024]{1,0:T(8,128)(2,1)S(1)}, u32[]{:S(2)}, u32[]{:S(2)}) collective-permute-start(bf16[8,1024]{1,0:T(8,128)(2,1)S(1)} %collective-permute-done), channel_id=1, source_target_pairs={{0,8},{8,16},{16,24},{24,32},{32,40},{40,48},{48,56},{56,64},{64,7... | collective-permute-start | bytes 49160 | tf_op jit(solution)/shard_map/ppermute | solution.py:18
  48.9 4.4 %copy-start.2 = (s32[4]{0:T(128)S(1)}, s32[4]{0:T(128)}, u32[]{:S(2)}) copy-start(s32[4]{0:T(128)} %param.15) | copy-start | bytes 52
  65.7 5.4 %collective-permute-start.2 = (f32[8]{0:T(128)S(1)}, f32[8]{0:T(128)S(1)}, u32[]{:S(2)}, u32[]{:S(2)}) collective-permute-start(f32[8]{0:T(128)S(1)} %slice_bitcast_fusion), channel_id=1, source_target_pairs={{0,1016},{8,0},{16,8},{24,16},{32,24},{40,32},{48,40},{56,48},{64,... | collective-permute-start | bytes 104 | tf_op jit(solution)/shard_map/ppermute | solution.py:18
  71.1 6.8 %collective-permute-start.3 = (f32[8]{0:T(128)S(1)}, f32[8]{0:T(128)S(1)}, u32[]{:S(2)}, u32[]{:S(2)}) collective-permute-start(f32[8]{0:T(128)S(1)} %bitcast_add_fusion.1), channel_id=1, source_target_pairs={{0,1016},{8,0},{16,8},{24,16},{32,24},{40,32},{48,40},{56,48},{64,... | collective-permute-start | bytes 104 | tf_op jit(solution)/shard_map/ppermute | solution.py:18
where the time goes:
time: 78.8 us; the launch traced here: 78.5 us
  blocking collectives  25.3 us (32%)
  waiting for transfers between devices  22.5 us (29%)
  starting transfers between devices  13.2 us (17%)
  matrix products  12.2 us (15%)
  local copies, waits for them, and re-layouts  2.31 us (3%)
  other arithmetic  1.56 us (2%)
  between operations  1.42 us (2%)
    ppermute x4, waiting for transfers between devices, passed_along(): return lax.ppermute(value, axis, pairs)  22.5 us
    ppermute x4, starting transfers between devices, passed_along(): return lax.ppermute(value, axis, pairs)  13.2 us
    all_gather x1, blocking collectives, local(): lax.all_gather(band_slice, 'tm', axis=1, tiled=True)  13.2 us
    unnamed x1, blocking collectives  12.1 us
    dot_general x1, matrix products, local(): jnp.dot(attended.reshape(-1, feature_width), w_out, preferred_element_typ...  4.33 us
    dot_general x1, matrix products, local(): jnp.dot(frame_flat, w_key, preferred_element_type=jnp.float32)  3.17 us
    dot_general x1, matrix products, local(): jnp.einsum('tk,cfk->ctf', band_query, key_rows, preferred_element_type=jn...  2.79 us
    unnamed x15, local copies, waits for them, and re-layouts  1.98 us
  transfers between devices with their start and end apart: 4, of which 4 were waited for; matrix products, arithmetic and copies ran while one was open for 10% of the time, Pallas kernels for 0%

commit v1 on v0

v1 whole, which is shorter than its diff:
```python
import jax
import jax.numpy as jnp
from jax import lax
from jax.experimental import pallas as pl
from jax.experimental.pallas import tpu as pltpu
from jax.sharding import PartitionSpec as P

HOPS = 2
RING = 4
LOGIT_SCALE = 32.0
EPSILON = 1e-06
BOTH = ("dp", "tm")
F32 = jnp.float32
BF16 = jnp.bfloat16
ROWS = (((1,), (1,)), ((), ()))


def ring_groups(dp_count, tm_count):
    width = RING * tm_count
    return [list(range(g * width, (g + 1) * width)) for g in range(dp_count // RING)]


def moved(value, blocks):
    count = lax.axis_size("dp")
    pairs = [(source, (source + blocks) % count) for source in range(count)]
    return lax.ppermute(value, "dp", pairs)


def split_bf16(value):
    high = value.astype(BF16)
    return high, (value - high.astype(F32)).astype(BF16)


def score_kernel(
    place_ref, counts_ref, pos_ref, text_ref, key_ref, value_ref, gram_ref,
    similar_ref, loss_ref, terms_ref,
):
    clips, frames = gram_ref.shape[0], gram_ref.shape[1]
    texts = text_ref.shape[0]
    block = texts // RING
    place = place_ref[0]
    text = text_ref[...]
    scores = lax.dot_general(key_ref[...], text, ROWS, preferred_element_type=F32)
    inner_all = lax.dot_general(value_ref[...], text, ROWS, preferred_element_type=F32)
    text_wide = text.astype(F32)
    text_sq = jnp.sum((text_wide * text_wide).reshape(texts, -1, 128).sum(1).T, axis=0, keepdims=True)
    lane = lax.broadcasted_iota(jnp.int32, (1, texts), 1)
    hop = (place - lane // block + RING) % RING
    band_index = hop * block + lane % block
    in_band = hop <= HOPS
    frame_index = lax.broadcasted_iota(jnp.int32, (frames, texts), 0)
    terms = jnp.zeros((1, texts), F32)
    for clip in range(clips):
        rows = slice(clip * frames, (clip + 1) * frames)
        valid = frame_index < counts_ref[clip]
        score = jnp.where(valid, scores[rows], -jnp.inf)
        weights = jnp.exp(score - jnp.max(score, axis=0, keepdims=True))
        weights = weights * (1.0 / jnp.sum(weights, axis=0, keepdims=True))
        inner = jnp.sum(weights * inner_all[rows], axis=0, keepdims=True)
        w_high, w_low = split_bf16(weights)
        g_high, g_low = split_bf16(gram_ref[clip])
        mixed = (
            jnp.dot(g_high, w_high, preferred_element_type=F32)
            + jnp.dot(g_high, w_low, preferred_element_type=F32)
            + jnp.dot(g_low, w_high, preferred_element_type=F32)
        )
        pooled_sq = jnp.maximum(jnp.sum(weights * mixed, axis=0, keepdims=True), 0.0)
        similar = LOGIT_SCALE * inner / jnp.sqrt((pooled_sq + EPSILON) * (text_sq + EPSILON))
        for j in range(HOPS + 1):
            at = (place - j + RING) % RING
            part = similar[:, :block]
            for x in range(1, RING):
                part = jnp.where(at == x, similar[:, x * block:(x + 1) * block], part)
            similar_ref[clip, j:j + 1, :] = part
        exp_sims = jnp.where(in_band, jnp.exp(similar), 0.0)
        picked = jnp.sum(jnp.where(band_index == pos_ref[clip], similar, 0.0), axis=1, keepdims=True)
        total = jnp.sum(exp_sims, axis=1, keepdims=True)
        loss_ref[clip:clip + 1, :] = jnp.broadcast_to(jnp.log(total) - picked, (1, 128))
        terms = terms + exp_sims
    terms_ref[...] = jnp.broadcast_to(terms, terms_ref.shape)


def local(frames, texts, w_query, w_key, w_value, w_out, frame_counts, clip_pos):
    clips, frame_total, width = frames.shape
    slice_rows = texts.shape[0]
    tm_count = lax.axis_size("tm")
    groups = ring_groups(lax.axis_size("dp"), tm_count)
    peers = RING * tm_count
    block_rows = slice_rows * tm_count
    place = lax.axis_index("dp") % RING

    before = moved(texts, RING)
    target = jnp.arange(RING, dtype=jnp.int32)[:, None, None, None]
    outgoing = jnp.where(target >= place, texts[None, None], before[None, None])
    outgoing = jnp.broadcast_to(outgoing, (RING, tm_count, slice_rows, width))
    band_text = lax.all_to_all(
        outgoing.reshape(peers, slice_rows, width), BOTH, 0, 0, axis_index_groups=groups, tiled=True
    ).reshape(peers * slice_rows, width)

    flat = frames.reshape(-1, width)
    key_rows = jnp.dot(flat, w_key, preferred_element_type=F32).astype(BF16)
    key_rows = lax.dot_general(key_rows, w_query, ROWS, preferred_element_type=F32)
    key_rows = (key_rows * (width ** -0.5)).astype(BF16)
    value_rows = jnp.dot(flat, w_value, preferred_element_type=F32).astype(BF16)
    value_rows = jnp.dot(value_rows, w_out, preferred_element_type=F32).astype(BF16)
    by_clip = value_rows.reshape(clips, frame_total, width)
    gram = jnp.einsum("cfk,cgk->cfg", by_clip, by_clip, preferred_element_type=F32)

    smem = pl.BlockSpec(memory_space=pltpu.SMEM)
    vmem = pl.BlockSpec(memory_space=pltpu.VMEM)
    similar, loss, terms = pl.pallas_call(
        score_kernel,
        in_specs=[smem] * 3 + [vmem] * 4,
        out_specs=[vmem] * 3,
        out_shape=[
            jax.ShapeDtypeStruct((clips, HOPS + 1, block_rows), F32),
            jax.ShapeDtypeStruct((clips, 128), F32),
            jax.ShapeDtypeStruct((peers, peers * slice_rows), F32),
        ],
        compiler_params=pltpu.CompilerParams(vmem_limit_bytes=24 * 1024 * 1024),
        cost_estimate=pl.CostEstimate(flops=500_000_000, bytes_accessed=3_000_000, transcendentals=120_000),
    )(place.reshape(1), frame_counts, clip_pos, band_text, key_rows, value_rows, gram)

    met = lax.all_to_all(terms, BOTH, 0, 0, axis_index_groups=groups, tiled=True)
    home = (place * tm_count + lax.axis_index("tm")) * slice_rows
    met = lax.dynamic_slice_in_dim(met, home, slice_rows, axis=1).reshape(RING, tm_count, slice_rows)
    own = (jnp.arange(RING, dtype=jnp.int32) >= place)[:, None, None]
    own_sum = jnp.sum(jnp.where(own, met, 0.0), axis=(0, 1))
    before_sum = jnp.sum(jnp.where(own, 0.0, met), axis=(0, 1))
    text_lse = jnp.log(own_sum + moved(before_sum, -RING))
    return (similar, loss[:, 0], text_lse)


def solution(mesh):
    in_specs = (
        P(BOTH, None, None), P(BOTH, None), P(), P(), P(), P(), P(BOTH), P(BOTH),
    )
    out_specs = (P(BOTH, None, None), P(BOTH), P(BOTH))
    return jax.shard_map(local, mesh=mesh, in_specs=in_specs, out_specs=out_specs, check_vma=False)
```

time: 78.8 us -> 63.7 us (0.81)
  the two profiles are of different devices: /device:TPU:8 before, /device:TPU:1 now
where the time goes in v1:
time: 63.7 us; the launch traced here: 63.3 us
  waiting for transfers between devices  24.5 us (38%)
  starting transfers between devices  20.4 us (32%)
  matrix products  9.86 us (15%)
  local copies, waits for them, and re-layouts  5.06 us (8%)
  Pallas kernels  2.09 us (3%)
  between operations  0.74 us (1%)
  other arithmetic  0.69 us (1%)
    ppermute x2, waiting for transfers between devices, moved(): return lax.ppermute(value, 'dp', pairs)  13.2 us
    all_to_all x1, starting transfers between devices, local(): lax.all_to_all(outgoing.reshape(peers, slice_rows, width), BOTH, 0, 0, ax...  8.63 us
    ppermute x2, starting transfers between devices, moved(): return lax.ppermute(value, 'dp', pairs)  8.14 us
    all_to_all x1, waiting for transfers between devices, local(): lax.all_to_all(terms, BOTH, 0, 0, axis_index_groups=groups, tiled=True)  6.04 us
    all_to_all x1, waiting for transfers between devices, local(): lax.all_to_all(outgoing.reshape(peers, slice_rows, width), BOTH, 0, 0, ax...  5.23 us
    dot_general x1, matrix products, local(): lax.dot_general(key_rows, w_query, ROWS, preferred_element_type=F32)  5.18 us
    all_to_all x1, starting transfers between devices, local(): lax.all_to_all(terms, BOTH, 0, 0, axis_index_groups=groups, tiled=True)  3.65 us
    dot_general x1, matrix products, local(): jnp.dot(value_rows, w_out, preferred_element_type=F32).astype(BF16)  3.64 us
  transfers between devices with their start and end apart: 4, of which 4 were waited for; matrix products, arithmetic and copies ran while one was open for 18% of the time, Pallas kernels for 0%

profile of v1, /device:TPU:1, one launch (start us, length us, event | category | flops | bytes accessed | tf_op | source)
XLA Modules:
  0.0 63.3 jit_solution(7750035259205053070)
XLA Ops:
  0.6 0.0 copy-start
  0.6 4.5 %collective-permute-start = (bf16[8,1024]{1,0:T(8,128)(2,1)}, bf16[8,1024]{1,0:T(8,128)(2,1)S(1)}, u32[]{:S(2)}, u32[]{:S(2)}) collective-permute-start(bf16[8,1024]{1,0:T(8,128)(2,1)} %param.9), channel_id=1, source_target_pairs={{0,32},{8,40},{16,48},{24,56},{32,64},{40,72},{48,80},{56,88},{64,... | collective-permute-start | bytes 49160 | tf_op jit(solution)/shard_map/ppermute | solution.py:26
  5.2 0.0 copy-done
  5.2 0.0 copy-start.5
  5.2 3.6 %convolution_convert_fusion.value_ref = bf16[384,1024]{1,0:T(8,128)(2,1)S(1)} fusion(bf16[1024,1024]{1,0:T(8,128)(2,1)S(1)} %copy-done, bf16[384,1024]{1,0:T(8,128)(2,1)} %bitcast.20, bf16[1024,1024]{1,0:T(8,128)(2,1)} %param.12), kind=kOutput, calls=%fused_computation.1 | convolution fusion | flops 1611399168 | bytes 5767168 | tf_op jit(solution)/shard_map/dot_general | solution.py:105
  8.9 12.5 %collective-permute-done = bf16[8,1024]{1,0:T(8,128)(2,1)S(1)} collective-permute-done((bf16[8,1024]{1,0:T(8,128)(2,1)}, bf16[8,1024]{1,0:T(8,128)(2,1)S(1)}, u32[]{:S(2)}, u32[]{:S(2)}) %collective-permute-start) | collective-permute-done | bytes 16416 | tf_op jit(solution)/shard_map/ppermute | solution.py:26
  21.3 0.0 copy-done.5
  21.3 0.1 broadcast_select_fusion
  21.4 0.9 %broadcast_in_dim.60 = bf16[4,8,8,1024]{3,2,1,0:T(8,128)(2,1)} broadcast(bf16[4,8,1024]{2,1,0:T(8,128)(2,1)S(1)} %broadcast_select_fusion), dimensions={0,2,3} | broadcast | bytes 589824 | tf_op jit(solution)/shard_map/broadcast_in_dim | solution.py:95
  22.3 8.6 %all-to-all-start = ((bf16[32,8,1024]{2,1,0:T(8,128)(2,1)}), bf16[32,8,1024]{2,1,0:T(8,128)(2,1)S(1)}, u32[]{:S(2)}, u32[]{:S(2)}) async-start(bf16[32,8,1024]{2,1,0:T(8,128)(2,1)} %bitcast.18), calls=%async_computation | async-start | bytes 1048576 | tf_op jit(solution)/shard_map/all_to_all | solution.py:96
  30.9 1.1 %fusion.gram_ref = f32[4,96,96]{2,1,0:T(8,128)} fusion(bf16[4,96,1024]{2,1,0:T(8,128)(2,1)S(1)} %bitcast.15), kind=kOutput, calls=%fused_computation.11 | convolution fusion | flops 75497472 | bytes 933888 | tf_op jit(solution)/shard_map/cfk,cgk->cfg/dot_general | solution.py:107
  32.0 0.1 broadcast_in_dim.61
  32.0 0.1 broadcast_in_dim.62
  32.1 0.0 copy-start.3
  32.1 0.0 copy-start.4
  32.1 5.2 %multiply_convert_fusion.key_ref = bf16[384,1024]{1,0:T(8,128)(2,1)} fusion(bf16[1024,1024]{1,0:T(8,128)(2,1)} %param.10, bf16[384,1024]{1,0:T(8,128)(2,1)} %bitcast.21, bf16[1024,1024]{1,0:T(8,128)(2,1)} %param.11), kind=kOutput, calls=%fused_computation | convolution fusion | flops 1611792384 | bytes 5767168 | tf_op jit(solution)/shard_map/dot_general | solution.py:102
  37.3 5.2 %all-to-all-done = bf16[32,8,1024]{2,1,0:T(8,128)(2,1)S(1)} async-done(((bf16[32,8,1024]{2,1,0:T(8,128)(2,1)}), bf16[32,8,1024]{2,1,0:T(8,128)(2,1)S(1)}, u32[]{:S(2)}, u32[]{:S(2)}) %all-to-all-start) | async-done | bytes 524320 | tf_op jit(solution)/shard_map/all_to_all | solution.py:96
  42.5 0.0 copy-done.3
  42.5 0.0 copy-done.4
  42.5 0.0 copy-start.1
  42.5 0.9 %copy-done.1 = f32[4,96,96]{2,1,0:T(8,128)S(1)} copy-done((f32[4,96,96]{2,1,0:T(8,128)S(1)}, f32[4,96,96]{2,1,0:T(8,128)}, u32[]{:S(2)}) %copy-start.1) | copy-done | bytes 147480
  43.5 0.0 copy-start.2
  43.5 1.1 %copy-done.2 = bf16[384,1024]{1,0:T(8,128)(2,1)S(1)} copy-done((bf16[384,1024]{1,0:T(8,128)(2,1)S(1)}, bf16[384,1024]{1,0:T(8,128)(2,1)}, u32[]{:S(2)}) %copy-start.2) | copy-done | bytes 786456
  44.6 2.1 %shard_map.103 = (f32[4,3,64]{2,1,0:T(4,128)S(1)}, f32[4,128]{1,0:T(4,128)S(1)}, f32[32,256]{1,0:T(8,128)S(1)}) custom-call(s32[1]{0:T(128)} %bitcast.place_ref, s32[4]{0:T(128)S(1)} %copy-done.3, s32[4]{0:T(128)S(1)} %copy-done.4, bf16[256,1024]{1,0:T(8,128)(2,1)S(1)} %bitcast.16, bf16[384,1024]{1,0:T(8,128)(2,1)S(1)} %copy-done.2, ...), custom_call_target="tpu_custom_call" | custom-call | flops 500000000 | bytes 3000000 | tf_op jit(solution)/shard_map/pallas_call | solution.py:111
  46.7 0.7 %copy.13 = f32[32,1,256]{2,1,0:T(1,128)} copy(f32[32,1,256]{2,0,1:T(8,128)S(1)} %bitcast.17) | data formatting | bytes 65536 | tf_op jit(solution)/shard_map/all_to_all | solution.py:124
  47.3 3.6 %all-to-all-start.1 = ((f32[32,1,256]{2,1,0:T(1,128)}), f32[32,1,256]{2,1,0:T(1,128)S(1)}, u32[]{:S(2)}, u32[]{:S(2)}) async-start(f32[32,1,256]{2,1,0:T(1,128)} %copy.13), calls=%async_computation.1 | async-start | bytes 65536 | tf_op jit(solution)/shard_map/all_to_all | solution.py:124
  51.0 0.6 slice_reduce_fusion
  51.6 0.6 copy.14
  52.2 6.0 %all-to-all-done.1 = f32[32,1,256]{2,1,0:T(1,128)S(1)} async-done(((f32[32,1,256]{2,1,0:T(1,128)}), f32[32,1,256]{2,1,0:T(1,128)S(1)}, u32[]{:S(2)}, u32[]{:S(2)}) %all-to-all-start.1) | async-done | bytes 32800 | tf_op jit(solution)/shard_map/all_to_all | solution.py:124
  58.3 0.1 constant_dynamic-slice_fusion
  58.4 0.1 select_reduce_fusion
  58.4 3.6 %collective-permute-start.1 = (f32[8]{0:T(128)S(1)}, f32[8]{0:T(128)S(1)}, u32[]{:S(2)}, u32[]{:S(2)}) collective-permute-start(f32[8]{0:T(128)S(1)} %get-tuple-element.18), channel_id=1, source_target_pairs={{0,992},{8,1000},{16,1008},{24,1016},{32,0},{40,8},{48,16},{56,24}... | collective-permute-start | bytes 104 | tf_op jit(solution)/shard_map/ppermute | solution.py:26
  62.1 0.7 %collective-permute-done.1 = f32[8]{0:T(128)S(1)} collective-permute-done((f32[8]{0:T(128)S(1)}, f32[8]{0:T(128)S(1)}, u32[]{:S(2)}, u32[]{:S(2)}) %collective-permute-start.1) | collective-permute-done | bytes 64 | tf_op jit(solution)/shard_map/ppermute | solution.py:26
  62.8 0.5 add_log_fusion
  (1 shorter events, 0.0 us)
Async XLA Ops:
  0.6 4.5 %copy-start = (bf16[1024,1024]{1,0:T(8,128)(2,1)S(1)}, bf16[1024,1024]{1,0:T(8,128)(2,1)}, u32[]{:S(2)}) copy-start(bf16[1024,1024]{1,0:T(8,128)(2,1)} %param.13) | copy-start | bytes 6291460
  0.6 20.7 %collective-permute-start = (bf16[8,1024]{1,0:T(8,128)(2,1)}, bf16[8,1024]{1,0:T(8,128)(2,1)S(1)}, u32[]{:S(2)}, u32[]{:S(2)}) collective-permute-start(bf16[8,1024]{1,0:T(8,128)(2,1)} %param.9), channel_id=1, source_target_pairs={{0,32},{8,40},{16,48},{24,56},{32,64},{40,72},{48,80},{56,88},{64,... | collective-permute-start | bytes 49160 | tf_op jit(solution)/shard_map/ppermute | solution.py:26
  5.2 16.2 %copy-start.5 = (bf16[8,1024]{1,0:T(8,128)(2,1)S(1)}, bf16[8,1024]{1,0:T(8,128)(2,1)}, u32[]{:S(2)}) copy-start(bf16[8,1024]{1,0:T(8,128)(2,1)} %param.9) | copy-start | bytes 49156
  22.3 20.3 %all-to-all-start = ((bf16[32,8,1024]{2,1,0:T(8,128)(2,1)}), bf16[32,8,1024]{2,1,0:T(8,128)(2,1)S(1)}, u32[]{:S(2)}, u32[]{:S(2)}) async-start(bf16[32,8,1024]{2,1,0:T(8,128)(2,1)} %bitcast.18), calls=%async_computation | async-start | bytes 1048576 | tf_op jit(solution)/shard_map/all_to_all | solution.py:96
  32.1 10.4 %copy-start.3 = (s32[4]{0:T(128)S(1)}, s32[4]{0:T(128)}, u32[]{:S(2)}) copy-start(s32[4]{0:T(128)} %counts_ref.1) | copy-start | bytes 52
  32.1 10.4 %copy-start.4 = (s32[4]{0:T(128)S(1)}, s32[4]{0:T(128)}, u32[]{:S(2)}) copy-start(s32[4]{0:T(128)} %pos_ref.1) | copy-start | bytes 52
  42.5 0.9 %copy-start.1 = (f32[4,96,96]{2,1,0:T(8,128)S(1)}, f32[4,96,96]{2,1,0:T(8,128)}, u32[]{:S(2)}) copy-start(f32[4,96,96]{2,1,0:T(8,128)} %fusion.gram_ref) | copy-start | bytes 442372
  43.5 1.1 %copy-start.2 = (bf16[384,1024]{1,0:T(8,128)(2,1)S(1)}, bf16[384,1024]{1,0:T(8,128)(2,1)}, u32[]{:S(2)}) copy-start(bf16[384,1024]{1,0:T(8,128)(2,1)} %multiply_convert_fusion.key_ref) | copy-start | bytes 2359300
  47.3 10.9 %all-to-all-start.1 = ((f32[32,1,256]{2,1,0:T(1,128)}), f32[32,1,256]{2,1,0:T(1,128)S(1)}, u32[]{:S(2)}, u32[]{:S(2)}) async-start(f32[32,1,256]{2,1,0:T(1,128)} %copy.13), calls=%async_computation.1 | async-start | bytes 65536 | tf_op jit(solution)/shard_map/all_to_all | solution.py:124
  58.4 4.3 %collective-permute-start.1 = (f32[8]{0:T(128)S(1)}, f32[8]{0:T(128)S(1)}, u32[]{:S(2)}, u32[]{:S(2)}) collective-permute-start(f32[8]{0:T(128)S(1)} %get-tuple-element.18), channel_id=1, source_target_pairs={{0,992},{8,1000},{16,1008},{24,1016},{32,0},{40,8},{48,16},{56,24}... | collective-permute-start | bytes 104 | tf_op jit(solution)/shard_map/ppermute | solution.py:26

commit v2 on v1

v2 whole, which is shorter than its diff:
```python
import jax
import jax.numpy as jnp
from jax import lax
from jax.experimental import pallas as pl
from jax.experimental.pallas import tpu as pltpu
from jax.sharding import PartitionSpec as P

HOPS = 2
PAIR = 2
LOGIT_SCALE = 32.0
EPSILON = 1e-06
SLICE = 8
BOTH = ("dp", "tm")
F32 = jnp.float32
BF16 = jnp.bfloat16
ROWS = (((1,), (1,)), ((), ()))


def pair_groups(dp_count, tm_count):
    width = PAIR * tm_count
    return [list(range(g * width, (g + 1) * width)) for g in range(dp_count // PAIR)]


def moved(value, blocks):
    count = lax.axis_size("dp")
    pairs = [(source, (source + blocks) % count) for source in range(count)]
    return lax.ppermute(value, "dp", pairs)


def split_bf16(value):
    high = value.astype(BF16)
    return high, (value - high.astype(F32)).astype(BF16)


def project_kernel(
    frames_hbm, key_hbm, query_hbm, value_hbm, out_hbm,
    key_ref, value_ref, gram_ref,
    frames_ref, value_weight, out_weight, key_weight, query_weight, rows_ref, sems,
):
    clips, count = gram_ref.shape[0], gram_ref.shape[1]
    scale = frames_ref.shape[1] ** -0.5
    loads = [
        pltpu.make_async_copy(source, held, sems.at[at])
        for at, (source, held) in enumerate((
            (frames_hbm, frames_ref), (value_hbm, value_weight), (out_hbm, out_weight),
            (key_hbm, key_weight), (query_hbm, query_weight),
        ))
    ]
    for load in loads:
        load.start()
    loads[0].wait()
    loads[1].wait()
    rows_ref[...] = jnp.dot(frames_ref[...], value_weight[...], preferred_element_type=F32).astype(BF16)
    loads[2].wait()
    value_ref[...] = jnp.dot(rows_ref[...], out_weight[...], preferred_element_type=F32).astype(BF16)
    loads[3].wait()
    rows_ref[...] = jnp.dot(frames_ref[...], key_weight[...], preferred_element_type=F32).astype(BF16)
    for clip in range(clips):
        own = value_ref[clip * count:(clip + 1) * count, :]
        gram_ref[clip] = lax.dot_general(own, own, ROWS, preferred_element_type=F32)
    loads[4].wait()
    keys = lax.dot_general(rows_ref[...], query_weight[...], ROWS, preferred_element_type=F32)
    key_ref[...] = (keys * scale).astype(BF16)


def score_kernel(
    place_ref, counts_ref, pos_ref, text_ref, key_ref, value_ref, gram_ref,
    similar_ref, loss_ref, terms_ref,
):
    clips, frames = gram_ref.shape[0], gram_ref.shape[1]
    texts = text_ref.shape[0]
    block = texts // (2 * PAIR)
    place = place_ref[0]
    text = text_ref[...]
    scores = lax.dot_general(key_ref[...], text, ROWS, preferred_element_type=F32)
    inner_all = lax.dot_general(value_ref[...], text, ROWS, preferred_element_type=F32)
    text_wide = text.astype(F32)
    sq_high, sq_low = split_bf16(text_wide * text_wide)
    ones = jnp.ones((8, text.shape[1]), BF16)
    text_sq = lax.dot_general(ones, sq_high, ROWS, preferred_element_type=F32)
    text_sq = (text_sq + lax.dot_general(ones, sq_low, ROWS, preferred_element_type=F32))[:1]
    frame_index = lax.broadcasted_iota(jnp.int32, (frames, texts), 0)
    clip_index = lax.broadcasted_iota(jnp.int32, (clips, texts), 0)
    inner = jnp.zeros((clips, texts), F32)
    pooled_sq = jnp.zeros((clips, texts), F32)
    position = jnp.zeros((clips, texts), jnp.int32)
    for clip in range(clips):
        rows = slice(clip * frames, (clip + 1) * frames)
        valid = frame_index < counts_ref[clip]
        score = jnp.where(valid, scores[rows], -jnp.inf)
        weights = jnp.exp(score - jnp.max(score, axis=0, keepdims=True))
        weights = weights * (1.0 / jnp.sum(weights, axis=0, keepdims=True))
        w_high, w_low = split_bf16(weights)
        g_high, g_low = split_bf16(gram_ref[clip])
        mixed = (
            jnp.dot(g_high, w_high, preferred_element_type=F32)
            + jnp.dot(g_high, w_low, preferred_element_type=F32)
            + jnp.dot(g_low, w_high, preferred_element_type=F32)
        )
        here = clip_index == clip
        inner = jnp.where(here, jnp.sum(weights * inner_all[rows], axis=0, keepdims=True), inner)
        pooled_sq = jnp.where(here, jnp.sum(weights * mixed, axis=0, keepdims=True), pooled_sq)
        position = jnp.where(here, pos_ref[clip], position)
    pooled_sq = jnp.maximum(pooled_sq, 0.0)
    similar = LOGIT_SCALE * inner / jnp.sqrt((pooled_sq + EPSILON) * (text_sq + EPSILON))
    lane = lax.broadcasted_iota(jnp.int32, (clips, texts), 1)
    older = lane // SLICE % 2
    hop = place - lane // (2 * block) + 2 * older
    in_block = lane // (2 * SLICE) * SLICE % block + lane % SLICE
    exp_sims = jnp.where((hop >= 0) & (hop <= HOPS), jnp.exp(similar), 0.0)
    terms_ref[...] = jnp.sum(exp_sims, axis=0, keepdims=True)
    similar_ref[...] = similar
    hit = (hop >= 0) & (hop <= HOPS) & (hop * block + in_block == position)
    picked = jnp.sum(jnp.where(hit, similar, 0.0), axis=1, keepdims=True)
    total = jnp.sum(exp_sims, axis=1, keepdims=True)
    loss_ref[...] = jnp.broadcast_to(jnp.log(total) - picked, loss_ref.shape)


def local(frames, texts, w_query, w_key, w_value, w_out, frame_counts, clip_pos):
    clips, frame_total, width = frames.shape
    slice_rows = texts.shape[0]
    tm_count = lax.axis_size("tm")
    groups = pair_groups(lax.axis_size("dp"), tm_count)
    peers = PAIR * tm_count
    block_rows = slice_rows * tm_count
    place = lax.axis_index("dp") % PAIR

    both = jnp.concatenate([texts, moved(texts, 2)], axis=0)
    smem = pl.BlockSpec(memory_space=pltpu.SMEM)
    vmem = pl.BlockSpec(memory_space=pltpu.VMEM)
    rows = clips * frame_total
    key_rows, value_rows, gram = pl.pallas_call(
        project_kernel,
        in_specs=[pl.BlockSpec(memory_space=pltpu.HBM)] * 5,
        out_specs=[vmem] * 3,
        out_shape=[
            jax.ShapeDtypeStruct((rows, width), BF16),
            jax.ShapeDtypeStruct((rows, width), BF16),
            jax.ShapeDtypeStruct((clips, frame_total, frame_total), F32),
        ],
        scratch_shapes=[
            pltpu.VMEM((rows, width), BF16),
            *[pltpu.VMEM((width, width), BF16)] * 4,
            pltpu.VMEM((rows, width), BF16),
            pltpu.SemaphoreType.DMA((5,)),
        ],
        compiler_params=pltpu.CompilerParams(vmem_limit_bytes=52 * 1024 * 1024),
        cost_estimate=pl.CostEstimate(
            flops=8 * rows * width * width, bytes_accessed=8 * width * width, transcendentals=0
        ),
    )(frames.reshape(rows, width), w_key, w_query, w_value, w_out)

    band_text = lax.all_to_all(
        jnp.broadcast_to(both[None], (peers, 2 * slice_rows, width)),
        BOTH, 0, 0, axis_index_groups=groups, tiled=True,
    ).reshape(2 * peers * slice_rows, width)

    similar, loss, terms = pl.pallas_call(
        score_kernel,
        in_specs=[smem] * 3 + [vmem] * 4,
        out_specs=[vmem] * 3,
        out_shape=[
            jax.ShapeDtypeStruct((clips, 2 * peers * slice_rows), F32),
            jax.ShapeDtypeStruct((clips, 128), F32),
            jax.ShapeDtypeStruct((1, 2 * peers * slice_rows), F32),
        ],
        compiler_params=pltpu.CompilerParams(vmem_limit_bytes=24 * 1024 * 1024),
        cost_estimate=pl.CostEstimate(flops=500_000_000, bytes_accessed=3_000_000, transcendentals=120_000),
    )(place.reshape(1), frame_counts, clip_pos, band_text, key_rows, value_rows, gram)

    beyond = moved(terms, -2)
    lane = lax.broadcasted_iota(jnp.int32, terms.shape, 1)
    met = jnp.where(lane // slice_rows % 2 == 0, terms, beyond)
    similar, loss, met = lax.optimization_barrier((similar, loss, met))
    met = jnp.broadcast_to(met[None], (peers,) + met.shape)
    met = lax.all_to_all(met, BOTH, 0, 0, axis_index_groups=groups, tiled=True)
    home = (place * tm_count + lax.axis_index("tm")) * 2 * slice_rows
    met = lax.dynamic_slice_in_dim(jnp.sum(met, axis=(0, 1)), home, 2 * slice_rows)
    text_lse = jnp.log(met[:slice_rows] + met[slice_rows:])

    similar = similar.reshape(clips, PAIR, tm_count, 2, slice_rows)

    def part(which, older):
        return similar[:, which, :, older, :].reshape(clips, block_rows)

    first = place == 0
    by_hop = [
        jnp.where(first, part(0, 0), part(1, 0)),
        jnp.where(first, part(1, 1), part(0, 0)),
        jnp.where(first, part(0, 1), part(1, 1)),
    ]
    return (jnp.stack(by_hop, axis=1), loss[:, 0], text_lse)


def solution(mesh):
    in_specs = (
        P(BOTH, None, None), P(BOTH, None), P(), P(), P(), P(), P(BOTH), P(BOTH),
    )
    out_specs = (P(BOTH, None, None), P(BOTH), P(BOTH))
    return jax.shard_map(local, mesh=mesh, in_specs=in_specs, out_specs=out_specs, check_vma=False)
```

time: 63.7 us -> 62.1 us (0.975)
  matrix products: 9.86 us -> 0 us
  Pallas kernels: 2.09 us -> 7.72 us
  local copies, waits for them, and re-layouts: 5.06 us -> 2.55 us
  starting transfers between devices: 20.4 us -> 22.6 us
  waiting for transfers between devices: 24.5 us -> 26 us
  other arithmetic: 0.69 us -> 2.12 us
    dot_general x3 -> x0, matrix products: 9.86 us -> none  [the longest x1 5.18 us: local(): lax.dot_general(key_rows, w_query, ROWS, preferred_element_type=F32)]
    pallas_call x0 -> x1, Pallas kernels: none -> 6.06 us  [local(): pl.pallas_call(project_kernel, in_specs=[pl.BlockSpec(memory_space=pltpu....]
    ppermute x2, waiting for transfers between devices: 13.2 us -> 18.2 us  [moved(): return lax.ppermute(value, 'dp', pairs)]
    all_to_all x2, waiting for transfers between devices: 11.3 us -> 7.78 us  [the longest x1 4.07 us: local(): met = lax.all_to_all(met, BOTH, 0, 0, axis_index_groups=groups, tiled=True)]
    ppermute x2, starting transfers between devices: 8.14 us -> 11.2 us  [moved(): return lax.ppermute(value, 'dp', pairs)]
    unnamed x13 -> x4, local copies, waits for them, and re-layouts: 2.68 us -> 0.01 us
    all_to_all x2, starting transfers between devices: 12.3 us -> 11.4 us  [the longest x1 6.06 us: local(): lax.all_to_all(jnp.broadcast_to(both[None], (peers, 2 * slice_rows, width...]
    concatenate x0 -> x1, other arithmetic: none -> 0.72 us  [local(): both = jnp.concatenate([texts, moved(texts, 2)], axis=0)]
  transfers between devices with their start and end apart: 4 -> 4, of which waited for: 4 -> 4; matrix products, arithmetic and copies ran while one was open for 18% -> 3% of each run, Pallas kernels for 0% -> 10%
where the time goes in v2:
time: 62.1 us; the launch traced here: 61.7 us
  waiting for transfers between devices  26 us (42%)
  starting transfers between devices  22.6 us (36%)
  Pallas kernels  7.72 us (12%)
  local copies, waits for them, and re-layouts  2.55 us (4%)
  other arithmetic  2.12 us (3%)
  between operations  0.71 us (1%)
    ppermute x2, waiting for transfers between devices, moved(): return lax.ppermute(value, 'dp', pairs)  18.2 us
    ppermute x2, starting transfers between devices, moved(): return lax.ppermute(value, 'dp', pairs)  11.2 us
    pallas_call x1, Pallas kernels, local(): pl.pallas_call(project_kernel, in_specs=[pl.BlockSpec(memory_space=pltpu....  6.06 us
    all_to_all x1, starting transfers between devices, local(): lax.all_to_all(jnp.broadcast_to(both[None], (peers, 2 * slice_rows, width...  6.06 us
    all_to_all x1, starting transfers between devices, local(): met = lax.all_to_all(met, BOTH, 0, 0, axis_index_groups=groups, tiled=True)  5.32 us
    all_to_all x1, waiting for transfers between devices, local(): met = lax.all_to_all(met, BOTH, 0, 0, axis_index_groups=groups, tiled=True)  4.07 us
    all_to_all x1, waiting for transfers between devices, local(): lax.all_to_all(jnp.broadcast_to(both[None], (peers, 2 * slice_rows, width...  3.72 us
    pallas_call x1, Pallas kernels, local(): pl.pallas_call(score_kernel, in_specs=[smem] * 3 + [vmem] * 4, out_specs=...  1.66 us
  transfers between devices with their start and end apart: 4, of which 4 were waited for; matrix products, arithmetic and copies ran while one was open for 3% of the time, Pallas kernels for 10%

profile of v2, /device:TPU:1, one launch (start us, length us, event | category | flops | bytes accessed | tf_op | source)
XLA Modules:
  0.0 61.7 jit_solution(4365723592429730747)
XLA Ops:
  0.6 5.5 %collective-permute-start = (bf16[8,1024]{1,0:T(8,128)(2,1)}, bf16[8,1024]{1,0:T(8,128)(2,1)S(1)}, u32[]{:S(2)}, u32[]{:S(2)}) collective-permute-start(bf16[8,1024]{1,0:T(8,128)(2,1)} %param.9), channel_id=1, source_target_pairs={{0,16},{8,24},{16,32},{24,40},{32,48},{40,56},{48,64},{56,72},{64,... | collective-permute-start | bytes 49160 | tf_op jit(solution)/shard_map/ppermute | solution.py:27
  6.1 17.5 %collective-permute-done = bf16[8,1024]{1,0:T(8,128)(2,1)S(1)} collective-permute-done((bf16[8,1024]{1,0:T(8,128)(2,1)}, bf16[8,1024]{1,0:T(8,128)(2,1)S(1)}, u32[]{:S(2)}, u32[]{:S(2)}) %collective-permute-start) | collective-permute-done | bytes 16416 | tf_op jit(solution)/shard_map/ppermute | solution.py:27
  23.6 0.7 %pad_maximum_fusion = bf16[16,1024]{1,0:T(8,128)(2,1)S(1)} fusion(bf16[8,1024]{1,0:T(8,128)(2,1)S(1)} %collective-permute-done, bf16[8,1024]{1,0:T(8,128)(2,1)} %param.9), kind=kLoop, calls=%fused_computation | loop fusion | flops 65536 | bytes 65536 | tf_op jit(solution)/shard_map/concatenate | solution.py:128
  24.4 0.8 %broadcast_in_dim.6 = bf16[16,16,1024]{2,1,0:T(8,128)(2,1)} broadcast(bf16[16,1024]{1,0:T(8,128)(2,1)S(1)} %pad_maximum_fusion), dimensions={1,2} | broadcast | bytes 557056 | tf_op jit(solution)/shard_map/broadcast_in_dim | solution.py:154
  25.2 6.1 %all-to-all-start = ((bf16[16,16,1024]{2,1,0:T(8,128)(2,1)}), bf16[16,16,1024]{2,1,0:T(8,128)(2,1)S(1)}, u32[]{:S(2)}, u32[]{:S(2)}) async-start(bf16[16,16,1024]{2,1,0:T(8,128)(2,1)} %broadcast_in_dim.6), calls=%async_computation | async-start | bytes 1048576 | tf_op jit(solution)/shard_map/all_to_all | solution.py:153
  31.3 0.0 copy-start
  31.3 0.0 copy-start.1
  31.3 6.1 %shard_map.103 = (bf16[384,1024]{1,0:T(8,128)(2,1)S(1)}, bf16[384,1024]{1,0:T(8,128)(2,1)S(1)}, f32[4,96,96]{2,1,0:T(8,128)S(1)}) custom-call(bf16[384,1024]{1,0:T(8,128)(2,1)} %bitcast.6, bf16[1024,1024]{1,0:T(8,128)(2,1)} %key_hbm.1, bf16[1024,1024]{1,0:T(8,128)(2,1)} %query_hbm.1, bf16[1024,1024]{1,0:T(8,128)(2,1)} %value_hbm.1, bf16[1024,1024]{1,0:T(8,128)(2,1)} %out_hbm.1), custom_call_target="tpu_custom_call" | custom-call | flops 3221225472 | bytes 8388608 | tf_op jit(solution)/shard_map/pallas_call | solution.py:132
  37.4 3.7 %all-to-all-done = bf16[16,16,1024]{2,1,0:T(8,128)(2,1)S(1)} async-done(((bf16[16,16,1024]{2,1,0:T(8,128)(2,1)}), bf16[16,16,1024]{2,1,0:T(8,128)(2,1)S(1)}, u32[]{:S(2)}, u32[]{:S(2)}) %all-to-all-start) | async-done | bytes 524320 | tf_op jit(solution)/shard_map/all_to_all | solution.py:153
  41.1 0.0 copy-done
  41.1 0.0 copy-done.1
  41.1 1.7 %shard_map.104 = (f32[4,256]{1,0:T(4,128)S(1)}, f32[4,128]{1,0:T(4,128)S(1)}, f32[1,256]{1,0:T(1,128)S(1)}) custom-call(s32[1]{0:T(128)} %bitcast.place_ref, s32[4]{0:T(128)S(1)} %copy-done, s32[4]{0:T(128)S(1)} %copy-done.1, bf16[256,1024]{1,0:T(8,128)(2,1)S(1)} %bitcast.4, bf16[384,1024]{1,0:T(8,128)(2,1)S(1)} %get-tuple-element.12.key_ref, ...), custom_call_target="tpu_custom_call" | custom-call | flops 500000000 | bytes 3000000 | tf_op jit(solution)/shard_map/pallas_call | solution.py:158
  42.7 5.7 %collective-permute-start.1 = (f32[1,256]{1,0:T(1,128)S(1)}, f32[1,256]{1,0:T(1,128)S(1)}, u32[]{:S(2)}, u32[]{:S(2)}) collective-permute-start(f32[1,256]{1,0:T(1,128)S(1)} %get-tuple-element.17), channel_id=1, source_target_pairs={{0,1008},{8,1016},{16,0},{24,8},{32,16},{40,24},{48,32},{56,40},{6... | collective-permute-start | bytes 3080 | tf_op jit(solution)/shard_map/ppermute | solution.py:27
  48.5 0.7 %collective-permute-done.1 = f32[1,256]{1,0:T(1,128)S(1)} collective-permute-done((f32[1,256]{1,0:T(1,128)S(1)}, f32[1,256]{1,0:T(1,128)S(1)}, u32[]{:S(2)}, u32[]{:S(2)}) %collective-permute-start.1) | collective-permute-done | bytes 1056 | tf_op jit(solution)/shard_map/ppermute | solution.py:27
  49.2 0.6 broadcast_in_dim.16
  49.8 5.3 %all-to-all-start.1 = ((f32[16,1,256]{2,1,0:T(1,128)}), f32[16,1,256]{2,1,0:T(1,128)S(1)}, u32[]{:S(2)}, u32[]{:S(2)}) async-start(f32[16,1,256]{2,1,0:T(1,128)} %broadcast_in_dim.16), calls=%async_computation.1 | async-start | bytes 32768 | tf_op jit(solution)/shard_map/all_to_all | solution.py:176
  55.1 0.1 reshape.183
  55.3 0.2 fusion
  55.5 0.1 select_n.93
  55.5 0.1 select_n.95
  55.6 0.1 select_n.97
  55.7 0.6 pad_maximum_fusion.1
  56.3 0.6 %slice_reduce_fusion = f32[4]{0:T(128)} fusion(f32[4,128]{1,0:T(4,128)S(1)} %get-tuple-element.19), kind=kLoop, calls=%fused_computation.13 | loop fusion | bytes 32 | tf_op jit(solution)/shard_map/slice | solution.py:192
  56.9 4.1 %all-to-all-done.1 = f32[16,1,256]{2,1,0:T(1,128)S(1)} async-done(((f32[16,1,256]{2,1,0:T(1,128)}), f32[16,1,256]{2,1,0:T(1,128)S(1)}, u32[]{:S(2)}, u32[]{:S(2)}) %all-to-all-start.1) | async-done | bytes 16416 | tf_op jit(solution)/shard_map/all_to_all | solution.py:176
  61.0 0.1 dynamic_slice.3
  61.1 0.6 add_log_fusion
  (2 shorter events, 0.1 us)
Async XLA Ops:
  0.6 23.0 %collective-permute-start = (bf16[8,1024]{1,0:T(8,128)(2,1)}, bf16[8,1024]{1,0:T(8,128)(2,1)S(1)}, u32[]{:S(2)}, u32[]{:S(2)}) collective-permute-start(bf16[8,1024]{1,0:T(8,128)(2,1)} %param.9), channel_id=1, source_target_pairs={{0,16},{8,24},{16,32},{24,40},{32,48},{40,56},{48,64},{56,72},{64,... | collective-permute-start | bytes 49160 | tf_op jit(solution)/shard_map/ppermute | solution.py:27
  25.2 15.9 %all-to-all-start = ((bf16[16,16,1024]{2,1,0:T(8,128)(2,1)}), bf16[16,16,1024]{2,1,0:T(8,128)(2,1)S(1)}, u32[]{:S(2)}, u32[]{:S(2)}) async-start(bf16[16,16,1024]{2,1,0:T(8,128)(2,1)} %broadcast_in_dim.6), calls=%async_computation | async-start | bytes 1048576 | tf_op jit(solution)/shard_map/all_to_all | solution.py:153
  31.3 9.8 %copy-start = (s32[4]{0:T(128)S(1)}, s32[4]{0:T(128)}, u32[]{:S(2)}) copy-start(s32[4]{0:T(128)} %counts_ref.1) | copy-start | bytes 52
  31.3 9.8 %copy-start.1 = (s32[4]{0:T(128)S(1)}, s32[4]{0:T(128)}, u32[]{:S(2)}) copy-start(s32[4]{0:T(128)} %pos_ref.1) | copy-start | bytes 52
  42.7 6.5 %collective-permute-start.1 = (f32[1,256]{1,0:T(1,128)S(1)}, f32[1,256]{1,0:T(1,128)S(1)}, u32[]{:S(2)}, u32[]{:S(2)}) collective-permute-start(f32[1,256]{1,0:T(1,128)S(1)} %get-tuple-element.17), channel_id=1, source_target_pairs={{0,1008},{8,1016},{16,0},{24,8},{32,16},{40,24},{48,32},{56,40},{6... | collective-permute-start | bytes 3080 | tf_op jit(solution)/shard_map/ppermute | solution.py:27
  49.8 11.2 %all-to-all-start.1 = ((f32[16,1,256]{2,1,0:T(1,128)}), f32[16,1,256]{2,1,0:T(1,128)S(1)}, u32[]{:S(2)}, u32[]{:S(2)}) async-start(f32[16,1,256]{2,1,0:T(1,128)} %broadcast_in_dim.16), calls=%async_computation.1 | async-start | bytes 32768 | tf_op jit(solution)/shard_map/all_to_all | solution.py:176

commit v3 on v2

--- a/solution.py
+++ b/solution.py
@@ -125,7 +125,14 @@
     block_rows = slice_rows * tm_count
     place = lax.axis_index("dp") % PAIR
 
-    both = jnp.concatenate([texts, moved(texts, 2)], axis=0)
+    outgoing = lax.optimization_barrier(jnp.broadcast_to(texts[None, None], (peers, 2, slice_rows, width)))
+    before = jnp.broadcast_to(moved(texts, 2)[None, None], (peers, 1, slice_rows, width))
+    outgoing = lax.dynamic_update_slice(outgoing, before, (0, 1, 0, 0))
+    band_text = lax.all_to_all(
+        outgoing.reshape(peers, 2 * slice_rows, width),
+        BOTH, 0, 0, axis_index_groups=groups, tiled=True,
+    ).reshape(2 * peers * slice_rows, width)
+
     smem = pl.BlockSpec(memory_space=pltpu.SMEM)
     vmem = pl.BlockSpec(memory_space=pltpu.VMEM)
     rows = clips * frame_total
@@ -150,11 +157,6 @@
         ),
     )(frames.reshape(rows, width), w_key, w_query, w_value, w_out)
 
-    band_text = lax.all_to_all(
-        jnp.broadcast_to(both[None], (peers, 2 * slice_rows, width)),
-        BOTH, 0, 0, axis_index_groups=groups, tiled=True,
-    ).reshape(2 * peers * slice_rows, width)
-
     similar, loss, terms = pl.pallas_call(
         score_kernel,
         in_specs=[smem] * 3 + [vmem] * 4,
@@ -168,15 +170,12 @@
         cost_estimate=pl.CostEstimate(flops=500_000_000, bytes_accessed=3_000_000, transcendentals=120_000),
     )(place.reshape(1), frame_counts, clip_pos, band_text, key_rows, value_rows, gram)
 
-    beyond = moved(terms, -2)
-    lane = lax.broadcasted_iota(jnp.int32, terms.shape, 1)
-    met = jnp.where(lane // slice_rows % 2 == 0, terms, beyond)
-    similar, loss, met = lax.optimization_barrier((similar, loss, met))
-    met = jnp.broadcast_to(met[None], (peers,) + met.shape)
+    similar, loss, terms = lax.optimization_barrier((similar, loss, terms))
+    met = jnp.broadcast_to(terms[None], (peers,) + terms.shape)
     met = lax.all_to_all(met, BOTH, 0, 0, axis_index_groups=groups, tiled=True)
     home = (place * tm_count + lax.axis_index("tm")) * 2 * slice_rows
     met = lax.dynamic_slice_in_dim(jnp.sum(met, axis=(0, 1)), home, 2 * slice_rows)
-    text_lse = jnp.log(met[:slice_rows] + met[slice_rows:])
+    text_lse = jnp.log(met[:slice_rows] + moved(met[slice_rows:], -2))
 
     similar = similar.reshape(clips, PAIR, tm_count, 2, slice_rows)
 

time: 62.1 us -> 60.4 us (0.973)
  waiting for transfers between devices: 26 us -> 24.4 us
  local copies, waits for them, and re-layouts: 2.55 us -> 4.1 us
  starting transfers between devices: 22.6 us -> 21.7 us
  other arithmetic: 2.12 us -> 1.32 us
    ppermute x2, waiting for transfers between devices: 18.2 us -> 16.7 us  [moved(): return lax.ppermute(value, 'dp', pairs)]
    all_to_all x1, starting transfers between devices: 5.32 us -> 4.44 us  [local(): met = lax.all_to_all(met, BOTH, 0, 0, axis_index_groups=groups, tiled=True)]
    dynamic_update_slice x0 -> x1, local copies, waits for them, and re-layouts: none -> 0.74 us  [local(): outgoing = lax.dynamic_update_slice(outgoing, before, (0, 1, 0, 0))]
    broadcast_in_dim x2, local copies, waits for them, and re-layouts: 1.46 us -> 2.19 us  [the longest x1 1.58 us: local(): jnp.broadcast_to(texts[None, None], (peers, 2, slice_rows, width))]
    concatenate x1 -> x0, other arithmetic: 0.72 us -> none  [local(): both = jnp.concatenate([texts, moved(texts, 2)], axis=0)]
  transfers between devices with their start and end apart: 4 -> 4, of which waited for: 4 -> 4; matrix products, arithmetic and copies ran while one was open for 3% -> 6% of each run, Pallas kernels for 10% -> 10%
where the time goes in v3:
time: 60.4 us; the launch traced here: 60 us
  waiting for transfers between devices  24.4 us (40%)
  starting transfers between devices  21.7 us (36%)
  Pallas kernels  7.72 us (13%)
  local copies, waits for them, and re-layouts  4.1 us (7%)
  other arithmetic  1.32 us (2%)
  between operations  0.69 us (1%)
    ppermute x2, waiting for transfers between devices, moved(): return lax.ppermute(value, 'dp', pairs)  16.7 us
    ppermute x2, starting transfers between devices, moved(): return lax.ppermute(value, 'dp', pairs)  11.2 us
    pallas_call x1, Pallas kernels, local(): pl.pallas_call(project_kernel, in_specs=[pl.BlockSpec(memory_space=pltpu....  6.06 us
    all_to_all x1, starting transfers between devices, local(): lax.all_to_all(outgoing.reshape(peers, 2 * slice_rows, width), BOTH, 0, 0...  6.06 us
    all_to_all x1, starting transfers between devices, local(): met = lax.all_to_all(met, BOTH, 0, 0, axis_index_groups=groups, tiled=True)  4.44 us
    all_to_all x1, waiting for transfers between devices, local(): met = lax.all_to_all(met, BOTH, 0, 0, axis_index_groups=groups, tiled=True)  4.07 us
    all_to_all x1, waiting for transfers between devices, local(): lax.all_to_all(outgoing.reshape(peers, 2 * slice_rows, width), BOTH, 0, 0...  3.72 us
    pallas_call x1, Pallas kernels, local(): pl.pallas_call(score_kernel, in_specs=[smem] * 3 + [vmem] * 4, out_specs=...  1.66 us
  transfers between devices with their start and end apart: 4, of which 4 were waited for; matrix products, arithmetic and copies ran while one was open for 6% of the time, Pallas kernels for 10%

profile of v3, /device:TPU:1, one launch (start us, length us, event | category | flops | bytes accessed | tf_op | source)
XLA Modules:
  0.0 60.0 jit_solution(10008956294763060284)
XLA Ops:
  0.6 5.5 %collective-permute-start = (bf16[8,1024]{1,0:T(8,128)(2,1)}, bf16[8,1024]{1,0:T(8,128)(2,1)S(1)}, u32[]{:S(2)}, u32[]{:S(2)}) collective-permute-start(bf16[8,1024]{1,0:T(8,128)(2,1)} %param.9), channel_id=1, source_target_pairs={{0,16},{8,24},{16,32},{24,40},{32,48},{40,56},{48,64},{56,72},{64,... | collective-permute-start | bytes 49160 | tf_op jit(solution)/shard_map/ppermute | solution.py:27
  6.1 1.6 %broadcast_in_dim.8 = bf16[16,2,8,1024]{3,2,1,0:T(8,128)(2,1)} broadcast(bf16[8,1024]{1,0:T(8,128)(2,1)} %param.9), dimensions={2,3} | broadcast | bytes 540672 | tf_op jit(solution)/shard_map/broadcast_in_dim | solution.py:128
  7.7 16.0 %collective-permute-done = bf16[8,1024]{1,0:T(8,128)(2,1)S(1)} collective-permute-done((bf16[8,1024]{1,0:T(8,128)(2,1)}, bf16[8,1024]{1,0:T(8,128)(2,1)S(1)}, u32[]{:S(2)}, u32[]{:S(2)}) %collective-permute-start) | collective-permute-done | bytes 16416 | tf_op jit(solution)/shard_map/ppermute | solution.py:27
  23.6 0.7 %broadcast_dynamic-update-slice_fusion = bf16[16,2,8,1024]{3,2,1,0:T(8,128)(2,1)} fusion(bf16[16,2,8,1024]{3,2,1,0:T(8,128)(2,1)} %broadcast_in_dim.8, bf16[8,1024]{1,0:T(8,128)(2,1)S(1)} %collective-permute-done), kind=kLoop, calls=%fused_computation | loop fusion | bytes 278528 | tf_op jit(solution)/shard_map/dynamic_update_slice | solution.py:130
  24.4 6.1 %all-to-all-start = ((bf16[16,16,1024]{2,1,0:T(8,128)(2,1)}), bf16[16,16,1024]{2,1,0:T(8,128)(2,1)S(1)}, u32[]{:S(2)}, u32[]{:S(2)}) async-start(bf16[16,16,1024]{2,1,0:T(8,128)(2,1)} %bitcast.1), calls=%async_computation | async-start | bytes 1048576 | tf_op jit(solution)/shard_map/all_to_all | solution.py:131
  30.4 0.0 copy-start
  30.5 0.0 copy-start.1
  30.5 6.1 %shard_map.103 = (bf16[384,1024]{1,0:T(8,128)(2,1)S(1)}, bf16[384,1024]{1,0:T(8,128)(2,1)S(1)}, f32[4,96,96]{2,1,0:T(8,128)S(1)}) custom-call(bf16[384,1024]{1,0:T(8,128)(2,1)} %bitcast.7, bf16[1024,1024]{1,0:T(8,128)(2,1)} %key_hbm.1, bf16[1024,1024]{1,0:T(8,128)(2,1)} %query_hbm.1, bf16[1024,1024]{1,0:T(8,128)(2,1)} %value_hbm.1, bf16[1024,1024]{1,0:T(8,128)(2,1)} %out_hbm.1), custom_call_target="tpu_custom_call" | custom-call | flops 3221225472 | bytes 8388608 | tf_op jit(solution)/shard_map/pallas_call | solution.py:139
  36.5 3.7 %all-to-all-done = bf16[16,16,1024]{2,1,0:T(8,128)(2,1)S(1)} async-done(((bf16[16,16,1024]{2,1,0:T(8,128)(2,1)}), bf16[16,16,1024]{2,1,0:T(8,128)(2,1)S(1)}, u32[]{:S(2)}, u32[]{:S(2)}) %all-to-all-start) | async-done | bytes 524320 | tf_op jit(solution)/shard_map/all_to_all | solution.py:131
  40.2 0.0 copy-done
  40.2 0.0 copy-done.1
  40.3 1.7 %shard_map.104 = (f32[4,256]{1,0:T(4,128)S(1)}, f32[4,128]{1,0:T(4,128)S(1)}, f32[1,256]{1,0:T(1,128)S(1)}) custom-call(s32[1]{0:T(128)} %bitcast.place_ref, s32[4]{0:T(128)S(1)} %copy-done, s32[4]{0:T(128)S(1)} %copy-done.1, bf16[256,1024]{1,0:T(8,128)(2,1)S(1)} %bitcast.5, bf16[384,1024]{1,0:T(8,128)(2,1)S(1)} %get-tuple-element.9.key_ref, ...), custom_call_target="tpu_custom_call" | custom-call | flops 500000000 | bytes 3000000 | tf_op jit(solution)/shard_map/pallas_call | solution.py:160
  41.9 0.6 %broadcast_in_dim.11 = f32[16,1,256]{2,1,0:T(1,128)} broadcast(f32[256]{0:T(256)S(1)} %bitcast.6), dimensions={2} | broadcast | bytes 17408 | tf_op jit(solution)/shard_map/broadcast_in_dim | solution.py:174
  42.5 4.4 %all-to-all-start.1 = ((f32[16,1,256]{2,1,0:T(1,128)}), f32[16,1,256]{2,1,0:T(1,128)S(1)}, u32[]{:S(2)}, u32[]{:S(2)}) async-start(f32[16,1,256]{2,1,0:T(1,128)} %broadcast_in_dim.11), calls=%async_computation.1 | async-start | bytes 32768 | tf_op jit(solution)/shard_map/all_to_all | solution.py:175
  47.0 0.1 reshape.89
  47.1 0.2 fusion
  47.3 0.1 select_n.59
  47.4 0.1 select_n.61
  47.4 0.1 select_n.63
  47.5 0.6 %pad_maximum_fusion = f32[4,3,64]{2,0,1:T(4,128)} fusion(f32[4,1,64]{2,0,1:T(4,128)S(1)} %select_n.63, f32[4,1,64]{2,0,1:T(4,128)S(1)} %select_n.61, f32[4,1,64]{2,0,1:T(4,128)S(1)} %select_n.59), kind=kLoop, calls=%fused_computation.7 | loop fusion | flops 1536 | bytes 6144 | tf_op jit(solution)/shard_map/stack | solution.py:191
  48.1 0.6 %slice_reduce_fusion = f32[4]{0:T(128)} fusion(f32[4,128]{1,0:T(4,128)S(1)} %get-tuple-element.13), kind=kLoop, calls=%fused_computation.8 | loop fusion | bytes 32 | tf_op jit(solution)/shard_map/slice | solution.py:191
  48.8 4.1 %all-to-all-done.1 = f32[16,1,256]{2,1,0:T(1,128)S(1)} async-done(((f32[16,1,256]{2,1,0:T(1,128)}), f32[16,1,256]{2,1,0:T(1,128)S(1)}, u32[]{:S(2)}, u32[]{:S(2)}) %all-to-all-start.1) | async-done | bytes 16416 | tf_op jit(solution)/shard_map/all_to_all | solution.py:175
  52.9 0.1 dynamic_slice.3
  52.9 0.1 slice.29
  53.0 5.8 %collective-permute-start.1 = (f32[8]{0:T(128)S(1)}, f32[8]{0:T(128)S(1)}, u32[]{:S(2)}, u32[]{:S(2)}) collective-permute-start(f32[8]{0:T(128)S(1)} %slice.29), channel_id=1, source_target_pairs={{0,1008},{8,1016},{16,0},{24,8},{32,16},{40,24},{48,32},{56,40},{6... | collective-permute-start | bytes 104 | tf_op jit(solution)/shard_map/ppermute | solution.py:27
  58.8 0.7 %collective-permute-done.1 = f32[8]{0:T(128)S(1)} collective-permute-done((f32[8]{0:T(128)S(1)}, f32[8]{0:T(128)S(1)}, u32[]{:S(2)}, u32[]{:S(2)}) %collective-permute-start.1) | collective-permute-done | bytes 64 | tf_op jit(solution)/shard_map/ppermute | solution.py:27
  59.5 0.5 add_log_fusion
  (1 shorter events, 0.0 us)
Async XLA Ops:
  0.6 23.0 %collective-permute-start = (bf16[8,1024]{1,0:T(8,128)(2,1)}, bf16[8,1024]{1,0:T(8,128)(2,1)S(1)}, u32[]{:S(2)}, u32[]{:S(2)}) collective-permute-start(bf16[8,1024]{1,0:T(8,128)(2,1)} %param.9), channel_id=1, source_target_pairs={{0,16},{8,24},{16,32},{24,40},{32,48},{40,56},{48,64},{56,72},{64,... | collective-permute-start | bytes 49160 | tf_op jit(solution)/shard_map/ppermute | solution.py:27
  24.4 15.9 %all-to-all-start = ((bf16[16,16,1024]{2,1,0:T(8,128)(2,1)}), bf16[16,16,1024]{2,1,0:T(8,128)(2,1)S(1)}, u32[]{:S(2)}, u32[]{:S(2)}) async-start(bf16[16,16,1024]{2,1,0:T(8,128)(2,1)} %bitcast.1), calls=%async_computation | async-start | bytes 1048576 | tf_op jit(solution)/shard_map/all_to_all | solution.py:131
  30.4 9.8 %copy-start = (s32[4]{0:T(128)S(1)}, s32[4]{0:T(128)}, u32[]{:S(2)}) copy-start(s32[4]{0:T(128)} %counts_ref.1) | copy-start | bytes 52
  30.5 9.8 %copy-start.1 = (s32[4]{0:T(128)S(1)}, s32[4]{0:T(128)}, u32[]{:S(2)}) copy-start(s32[4]{0:T(128)} %pos_ref.1) | copy-start | bytes 52
  42.5 10.3 %all-to-all-start.1 = ((f32[16,1,256]{2,1,0:T(1,128)}), f32[16,1,256]{2,1,0:T(1,128)S(1)}, u32[]{:S(2)}, u32[]{:S(2)}) async-start(f32[16,1,256]{2,1,0:T(1,128)} %broadcast_in_dim.11), calls=%async_computation.1 | async-start | bytes 32768 | tf_op jit(solution)/shard_map/all_to_all | solution.py:175
  53.0 6.5 %collective-permute-start.1 = (f32[8]{0:T(128)S(1)}, f32[8]{0:T(128)S(1)}, u32[]{:S(2)}, u32[]{:S(2)}) collective-permute-start(f32[8]{0:T(128)S(1)} %slice.29), channel_id=1, source_target_pairs={{0,1008},{8,1016},{16,0},{24,8},{32,16},{40,24},{48,32},{56,40},{6... | collective-permute-start | bytes 104 | tf_op jit(solution)/shard_map/ppermute | solution.py:27

commit v4 on v3

--- a/solution.py
+++ b/solution.py
@@ -6,6 +6,7 @@
 from jax.sharding import PartitionSpec as P
 
 HOPS = 2
+RING = 4
 PAIR = 2
 LOGIT_SCALE = 32.0
 EPSILON = 1e-06
@@ -16,14 +17,14 @@
 ROWS = (((1,), (1,)), ((), ()))
 
 
-def pair_groups(dp_count, tm_count):
-    width = PAIR * tm_count
-    return [list(range(g * width, (g + 1) * width)) for g in range(dp_count // PAIR)]
-
-
-def moved(value, blocks):
+def block_groups(dp_count, tm_count, blocks):
+    width = blocks * tm_count
+    return [list(range(g * width, (g + 1) * width)) for g in range(dp_count // blocks)]
+
+
+def moved(value, blocks, places=range(RING)):
     count = lax.axis_size("dp")
-    pairs = [(source, (source + blocks) % count) for source in range(count)]
+    pairs = [(source, (source + blocks) % count) for source in range(count) if source % RING in places]
     return lax.ppermute(value, "dp", pairs)
 
 
@@ -120,7 +121,8 @@
     clips, frame_total, width = frames.shape
     slice_rows = texts.shape[0]
     tm_count = lax.axis_size("tm")
-    groups = pair_groups(lax.axis_size("dp"), tm_count)
+    dp_count = lax.axis_size("dp")
+    groups = block_groups(dp_count, tm_count, PAIR)
     peers = PAIR * tm_count
     block_rows = slice_rows * tm_count
     place = lax.axis_index("dp") % PAIR
@@ -171,11 +173,18 @@
     )(place.reshape(1), frame_counts, clip_pos, band_text, key_rows, value_rows, gram)
 
     similar, loss, terms = lax.optimization_barrier((similar, loss, terms))
-    met = jnp.broadcast_to(terms[None], (peers,) + terms.shape)
-    met = lax.all_to_all(met, BOTH, 0, 0, axis_index_groups=groups, tiled=True)
+    met = jnp.broadcast_to(terms[None], (RING * tm_count,) + terms.shape)
+    met = lax.all_to_all(
+        met, BOTH, 0, 0, axis_index_groups=block_groups(dp_count, tm_count, RING), tiled=True
+    )
+    met = jnp.sum(met.reshape(RING // PAIR, peers, -1), axis=1)
     home = (place * tm_count + lax.axis_index("tm")) * 2 * slice_rows
-    met = lax.dynamic_slice_in_dim(jnp.sum(met, axis=(0, 1)), home, 2 * slice_rows)
-    text_lse = jnp.log(met[:slice_rows] + moved(met[slice_rows:], -2))
+    met = lax.dynamic_slice_in_dim(met, home, 2 * slice_rows, axis=1)
+    later = lax.axis_index("dp") % RING >= PAIR
+    newer = jnp.where(later, met[1, :slice_rows], met[0, :slice_rows])
+    older = jnp.where(later, met[0, slice_rows:], met[1, slice_rows:])
+    beyond = moved(older, -RING, range(PAIR, RING))
+    text_lse = jnp.log(newer + jnp.where(later, beyond, older))
 
     similar = similar.reshape(clips, PAIR, tm_count, 2, slice_rows)
 

time: 60.4 us -> 59.1 us (0.978)
  the two profiles are of different devices: /device:TPU:1 before, /device:TPU:6 now
where the time goes in v4:
time: 59.1 us; the launch traced here: 58.7 us
  starting transfers between devices  35.3 us (60%)
  waiting for transfers between devices  9.5 us (16%)
  Pallas kernels  7.73 us (13%)
  local copies, waits for them, and re-layouts  4.04 us (7%)
  other arithmetic  1.45 us (2%)
  between operations  0.7 us (1%)
    all_to_all x1, starting transfers between devices, local(): lax.all_to_all(outgoing.reshape(peers, 2 * slice_rows, width), BOTH, 0, 0...  13.9 us
    all_to_all x1, starting transfers between devices, local(): lax.all_to_all(met, BOTH, 0, 0, axis_index_groups=block_groups(dp_count,...  11.9 us
    ppermute x2, starting transfers between devices, moved(): return lax.ppermute(value, 'dp', pairs)  9.53 us
    pallas_call x1, Pallas kernels, local(): pl.pallas_call(project_kernel, in_specs=[pl.BlockSpec(memory_space=pltpu....  6.06 us
    all_to_all x1, waiting for transfers between devices, local(): lax.all_to_all(met, BOTH, 0, 0, axis_index_groups=block_groups(dp_count,...  3.7 us
    all_to_all x1, waiting for transfers between devices, local(): lax.all_to_all(outgoing.reshape(peers, 2 * slice_rows, width), BOTH, 0, 0...  3.43 us
    ppermute x2, waiting for transfers between devices, moved(): return lax.ppermute(value, 'dp', pairs)  2.37 us
    pallas_call x1, Pallas kernels, local(): pl.pallas_call(score_kernel, in_specs=[smem] * 3 + [vmem] * 4, out_specs=...  1.67 us
  transfers between devices with their start and end apart: 4, of which 4 were waited for; matrix products, arithmetic and copies ran while one was open for 6% of the time, Pallas kernels for 10%

profile of v4, /device:TPU:6, one launch (start us, length us, event | category | flops | bytes accessed | tf_op | source)
XLA Modules:
  0.0 58.7 jit_solution(13059245106902923187)
XLA Ops:
  0.6 4.7 %collective-permute-start = (bf16[8,1024]{1,0:T(8,128)(2,1)}, bf16[8,1024]{1,0:T(8,128)(2,1)S(1)}, u32[]{:S(2)}, u32[]{:S(2)}) collective-permute-start(bf16[8,1024]{1,0:T(8,128)(2,1)} %param.9), channel_id=1, source_target_pairs={{0,16},{8,24},{16,32},{24,40},{32,48},{40,56},{48,64},{56,72},{64,... | collective-permute-start | bytes 49160 | tf_op jit(solution)/shard_map/ppermute | solution.py:28
  5.3 1.6 %broadcast_in_dim.8 = bf16[16,2,8,1024]{3,2,1,0:T(8,128)(2,1)} broadcast(bf16[8,1024]{1,0:T(8,128)(2,1)} %param.9), dimensions={2,3} | broadcast | bytes 540672 | tf_op jit(solution)/shard_map/broadcast_in_dim | solution.py:130
  6.9 1.1 %collective-permute-done = bf16[8,1024]{1,0:T(8,128)(2,1)S(1)} collective-permute-done((bf16[8,1024]{1,0:T(8,128)(2,1)}, bf16[8,1024]{1,0:T(8,128)(2,1)S(1)}, u32[]{:S(2)}, u32[]{:S(2)}) %collective-permute-start) | collective-permute-done | bytes 16416 | tf_op jit(solution)/shard_map/ppermute | solution.py:28
  8.0 0.7 %broadcast_dynamic-update-slice_fusion = bf16[16,2,8,1024]{3,2,1,0:T(8,128)(2,1)} fusion(bf16[16,2,8,1024]{3,2,1,0:T(8,128)(2,1)} %broadcast_in_dim.8, bf16[8,1024]{1,0:T(8,128)(2,1)S(1)} %collective-permute-done), kind=kLoop, calls=%fused_computation | loop fusion | bytes 278528 | tf_op jit(solution)/shard_map/dynamic_update_slice | solution.py:132
  8.7 13.9 %all-to-all-start = ((bf16[16,16,1024]{2,1,0:T(8,128)(2,1)}), bf16[16,16,1024]{2,1,0:T(8,128)(2,1)S(1)}, u32[]{:S(2)}, u32[]{:S(2)}) async-start(bf16[16,16,1024]{2,1,0:T(8,128)(2,1)} %bitcast.1), calls=%async_computation | async-start | bytes 1048576 | tf_op jit(solution)/shard_map/all_to_all | solution.py:133
  22.6 0.0 copy-start
  22.6 0.0 copy-start.1
  22.6 6.1 %shard_map.103 = (bf16[384,1024]{1,0:T(8,128)(2,1)S(1)}, bf16[384,1024]{1,0:T(8,128)(2,1)S(1)}, f32[4,96,96]{2,1,0:T(8,128)S(1)}) custom-call(bf16[384,1024]{1,0:T(8,128)(2,1)} %bitcast.19, bf16[1024,1024]{1,0:T(8,128)(2,1)} %key_hbm.1, bf16[1024,1024]{1,0:T(8,128)(2,1)} %query_hbm.1, bf16[1024,1024]{1,0:T(8,128)(2,1)} %value_hbm.1, bf16[1024,1024]{1,0:T(8,128)(2,1)} %out_hbm.1), custom_call_target="tpu_custom_call" | custom-call | flops 3221225472 | bytes 8388608 | tf_op jit(solution)/shard_map/pallas_call | solution.py:141
  28.7 3.4 %all-to-all-done = bf16[16,16,1024]{2,1,0:T(8,128)(2,1)S(1)} async-done(((bf16[16,16,1024]{2,1,0:T(8,128)(2,1)}), bf16[16,16,1024]{2,1,0:T(8,128)(2,1)S(1)}, u32[]{:S(2)}, u32[]{:S(2)}) %all-to-all-start) | async-done | bytes 524320 | tf_op jit(solution)/shard_map/all_to_all | solution.py:133
  32.1 0.0 copy-done
  32.1 0.0 copy-done.1
  32.1 1.7 %shard_map.104 = (f32[4,256]{1,0:T(4,128)S(1)}, f32[4,128]{1,0:T(4,128)S(1)}, f32[1,256]{1,0:T(1,128)S(1)}) custom-call(s32[1]{0:T(128)} %bitcast.place_ref, s32[4]{0:T(128)S(1)} %copy-done, s32[4]{0:T(128)S(1)} %copy-done.1, bf16[256,1024]{1,0:T(8,128)(2,1)S(1)} %bitcast.16, bf16[384,1024]{1,0:T(8,128)(2,1)S(1)} %get-tuple-element.9.key_ref, ...), custom_call_target="tpu_custom_call" | custom-call | flops 500000000 | bytes 3000000 | tf_op jit(solution)/shard_map/pallas_call | solution.py:162
  33.8 0.6 %broadcast_in_dim.11 = f32[32,1,256]{2,1,0:T(1,128)} broadcast(f32[256]{0:T(256)S(1)} %bitcast.17), dimensions={2} | broadcast | bytes 33792 | tf_op jit(solution)/shard_map/broadcast_in_dim | solution.py:176
  34.4 11.9 %all-to-all-start.1 = ((f32[32,1,256]{2,1,0:T(1,128)}), f32[32,1,256]{2,1,0:T(1,128)S(1)}, u32[]{:S(2)}, u32[]{:S(2)}) async-start(f32[32,1,256]{2,1,0:T(1,128)} %broadcast_in_dim.11), calls=%async_computation.1 | async-start | bytes 65536 | tf_op jit(solution)/shard_map/all_to_all | solution.py:177
  46.3 0.1 reshape.96
  46.5 0.2 fusion
  46.7 0.1 select_n.87
  46.7 0.1 select_n.89
  46.8 0.1 select_n.91
  46.9 0.6 %pad_maximum_fusion = f32[4,3,64]{2,0,1:T(4,128)} fusion(f32[4,1,64]{2,0,1:T(4,128)S(1)} %select_n.91, f32[4,1,64]{2,0,1:T(4,128)S(1)} %select_n.89, f32[4,1,64]{2,0,1:T(4,128)S(1)} %select_n.87), kind=kLoop, calls=%fused_computation.7 | loop fusion | flops 1536 | bytes 6144 | tf_op jit(solution)/shard_map/stack | solution.py:200
  47.5 0.6 %slice_reduce_fusion = f32[4]{0:T(128)} fusion(f32[4,128]{1,0:T(4,128)S(1)} %get-tuple-element.13), kind=kLoop, calls=%fused_computation.8 | loop fusion | bytes 32 | tf_op jit(solution)/shard_map/slice | solution.py:200
  48.1 3.7 %all-to-all-done.1 = f32[32,1,256]{2,1,0:T(1,128)S(1)} async-done(((f32[32,1,256]{2,1,0:T(1,128)}), f32[32,1,256]{2,1,0:T(1,128)S(1)}, u32[]{:S(2)}, u32[]{:S(2)}) %all-to-all-start.1) | async-done | bytes 32800 | tf_op jit(solution)/shard_map/all_to_all | solution.py:177
  51.9 0.1 constant_dynamic-slice_fusion
  51.9 0.1 fusion.6
  52.0 4.9 %collective-permute-start.1 = (f32[8]{0:T(128)S(1)}, f32[8]{0:T(128)S(1)}, u32[]{:S(2)}, u32[]{:S(2)}) collective-permute-start(f32[8]{0:T(128)S(1)} %fusion.6), channel_id=1, source_target_pairs={{16,1008},{24,1016},{48,16},{56,24},{80,48},{88,56},{112,80},{120,... | collective-permute-start | bytes 104 | tf_op jit(solution)/shard_map/ppermute | solution.py:28
  56.9 1.3 %collective-permute-done.1 = f32[8]{0:T(128)S(1)} collective-permute-done((f32[8]{0:T(128)S(1)}, f32[8]{0:T(128)S(1)}, u32[]{:S(2)}, u32[]{:S(2)}) %collective-permute-start.1) | collective-permute-done | bytes 64 | tf_op jit(solution)/shard_map/ppermute | solution.py:28
  58.2 0.6 %fusion.5 = f32[8]{0:T(128)} fusion(pred[]{:T(512)S(6)} %ge.3, f32[8]{0:T(128)S(1)} %collective-permute-done.1, f32[2,16]{1,0:T(2,128)S(1)} %constant_dynamic-slice_fusion), kind=kLoop, calls=%fused_computation.14 | loop fusion | flops 32 | bytes 1216 | tf_op jit(solution)/shard_map/log | solution.py:187
  (2 shorter events, 0.0 us)
Async XLA Ops:
  0.6 7.3 %collective-permute-start = (bf16[8,1024]{1,0:T(8,128)(2,1)}, bf16[8,1024]{1,0:T(8,128)(2,1)S(1)}, u32[]{:S(2)}, u32[]{:S(2)}) collective-permute-start(bf16[8,1024]{1,0:T(8,128)(2,1)} %param.9), channel_id=1, source_target_pairs={{0,16},{8,24},{16,32},{24,40},{32,48},{40,56},{48,64},{56,72},{64,... | collective-permute-start | bytes 49160 | tf_op jit(solution)/shard_map/ppermute | solution.py:28
  8.7 23.4 %all-to-all-start = ((bf16[16,16,1024]{2,1,0:T(8,128)(2,1)}), bf16[16,16,1024]{2,1,0:T(8,128)(2,1)S(1)}, u32[]{:S(2)}, u32[]{:S(2)}) async-start(bf16[16,16,1024]{2,1,0:T(8,128)(2,1)} %bitcast.1), calls=%async_computation | async-start | bytes 1048576 | tf_op jit(solution)/shard_map/all_to_all | solution.py:133
  22.6 9.5 %copy-start = (s32[4]{0:T(128)S(1)}, s32[4]{0:T(128)}, u32[]{:S(2)}) copy-start(s32[4]{0:T(128)} %counts_ref.1) | copy-start | bytes 52
  22.6 9.5 %copy-start.1 = (s32[4]{0:T(128)S(1)}, s32[4]{0:T(128)}, u32[]{:S(2)}) copy-start(s32[4]{0:T(128)} %pos_ref.1) | copy-start | bytes 52
  34.4 17.4 %all-to-all-start.1 = ((f32[32,1,256]{2,1,0:T(1,128)}), f32[32,1,256]{2,1,0:T(1,128)S(1)}, u32[]{:S(2)}, u32[]{:S(2)}) async-start(f32[32,1,256]{2,1,0:T(1,128)} %broadcast_in_dim.11), calls=%async_computation.1 | async-start | bytes 65536 | tf_op jit(solution)/shard_map/all_to_all | solution.py:177
  52.0 6.1 %collective-permute-start.1 = (f32[8]{0:T(128)S(1)}, f32[8]{0:T(128)S(1)}, u32[]{:S(2)}, u32[]{:S(2)}) collective-permute-start(f32[8]{0:T(128)S(1)} %fusion.6), channel_id=1, source_target_pairs={{16,1008},{24,1016},{48,16},{56,24},{80,48},{88,56},{112,80},{120,... | collective-permute-start | bytes 104 | tf_op jit(solution)/shard_map/ppermute | solution.py:28

commit v5 on v4

--- a/solution.py
+++ b/solution.py
@@ -106,7 +106,8 @@
     similar = LOGIT_SCALE * inner / jnp.sqrt((pooled_sq + EPSILON) * (text_sq + EPSILON))
     lane = lax.broadcasted_iota(jnp.int32, (clips, texts), 1)
     older = lane // SLICE % 2
-    hop = place - lane // (2 * block) + 2 * older
+    bringer = lane // (2 * block)
+    hop = place + jnp.where(older == 1, bringer + 1, -bringer)
     in_block = lane // (2 * SLICE) * SLICE % block + lane % SLICE
     exp_sims = jnp.where((hop >= 0) & (hop <= HOPS), jnp.exp(similar), 0.0)
     terms_ref[...] = jnp.sum(exp_sims, axis=0, keepdims=True)
@@ -128,7 +129,9 @@
     place = lax.axis_index("dp") % PAIR
 
     outgoing = lax.optimization_barrier(jnp.broadcast_to(texts[None, None], (peers, 2, slice_rows, width)))
-    before = jnp.broadcast_to(moved(texts, 2)[None, None], (peers, 1, slice_rows, width))
+    crossed = [(source, (source + (1 if source % PAIR else 3)) % dp_count) for source in range(dp_count)]
+    before = lax.ppermute(texts, "dp", crossed)
+    before = jnp.broadcast_to(before[None, None], (peers, 1, slice_rows, width))
     outgoing = lax.dynamic_update_slice(outgoing, before, (0, 1, 0, 0))
     band_text = lax.all_to_all(
         outgoing.reshape(peers, 2 * slice_rows, width),
@@ -178,11 +181,13 @@
         met, BOTH, 0, 0, axis_index_groups=block_groups(dp_count, tm_count, RING), tiled=True
     )
     met = jnp.sum(met.reshape(RING // PAIR, peers, -1), axis=1)
-    home = (place * tm_count + lax.axis_index("tm")) * 2 * slice_rows
-    met = lax.dynamic_slice_in_dim(met, home, 2 * slice_rows, axis=1)
+    mine = lax.axis_index("tm") * 2 * slice_rows
+    half = 2 * block_rows
+    newer = lax.dynamic_slice_in_dim(met, place * half + mine, slice_rows, axis=1)
+    older = lax.dynamic_slice_in_dim(met, (1 - place) * half + mine + slice_rows, slice_rows, axis=1)
     later = lax.axis_index("dp") % RING >= PAIR
-    newer = jnp.where(later, met[1, :slice_rows], met[0, :slice_rows])
-    older = jnp.where(later, met[0, slice_rows:], met[1, slice_rows:])
+    newer = jnp.where(later, newer[1], newer[0])
+    older = jnp.where(later, older[0], older[1])
     beyond = moved(older, -RING, range(PAIR, RING))
     text_lse = jnp.log(newer + jnp.where(later, beyond, older))
 
@@ -194,8 +199,8 @@
     first = place == 0
     by_hop = [
         jnp.where(first, part(0, 0), part(1, 0)),
-        jnp.where(first, part(1, 1), part(0, 0)),
-        jnp.where(first, part(0, 1), part(1, 1)),
+        jnp.where(first, part(0, 1), part(0, 0)),
+        jnp.where(first, part(1, 1), part(0, 1)),
     ]
     return (jnp.stack(by_hop, axis=1), loss[:, 0], text_lse)
 

time: 59.1 us -> 58.7 us (level)
  starting transfers between devices: 35.3 us -> 24.7 us
  waiting for transfers between devices: 9.5 us -> 19.8 us
    ppermute x0 -> x1, waiting for transfers between devices: none -> 11.6 us  [local(): before = lax.ppermute(texts, 'dp', crossed)]
    all_to_all x1, starting transfers between devices: 13.9 us -> 3.47 us  [local(): lax.all_to_all(outgoing.reshape(peers, 2 * slice_rows, width), BOTH, 0, 0...]
    ppermute x2 -> x1, starting transfers between devices: 9.53 us -> 4.85 us  [moved(): return lax.ppermute(value, 'dp', pairs)]
    ppermute x0 -> x1, starting transfers between devices: none -> 3.74 us  [local(): before = lax.ppermute(texts, 'dp', crossed)]
    ppermute x2 -> x1, waiting for transfers between devices: 2.37 us -> 1.27 us  [moved(): return lax.ppermute(value, 'dp', pairs)]
    all_to_all x1, starting transfers between devices: 11.9 us -> 12.6 us  [local(): lax.all_to_all(met, BOTH, 0, 0, axis_index_groups=block_groups(dp_count,...]
where the time goes in v5:
time: 58.7 us; the launch traced here: 58.3 us
  starting transfers between devices  24.7 us (42%)
  waiting for transfers between devices  19.8 us (34%)
  Pallas kernels  7.72 us (13%)
  local copies, waits for them, and re-layouts  4.05 us (7%)
  other arithmetic  1.31 us (2%)
  between operations  0.75 us (1%)
    all_to_all x1, starting transfers between devices, local(): lax.all_to_all(met, BOTH, 0, 0, axis_index_groups=block_groups(dp_count,...  12.6 us
    ppermute x1, waiting for transfers between devices, local(): before = lax.ppermute(texts, 'dp', crossed)  11.6 us
    pallas_call x1, Pallas kernels, local(): pl.pallas_call(project_kernel, in_specs=[pl.BlockSpec(memory_space=pltpu....  6.06 us
    ppermute x1, starting transfers between devices, moved(): return lax.ppermute(value, 'dp', pairs)  4.85 us
    ppermute x1, starting transfers between devices, local(): before = lax.ppermute(texts, 'dp', crossed)  3.74 us
    all_to_all x1, waiting for transfers between devices, local(): lax.all_to_all(met, BOTH, 0, 0, axis_index_groups=block_groups(dp_count,...  3.7 us
    all_to_all x1, starting transfers between devices, local(): lax.all_to_all(outgoing.reshape(peers, 2 * slice_rows, width), BOTH, 0, 0...  3.47 us
    all_to_all x1, waiting for transfers between devices, local(): lax.all_to_all(outgoing.reshape(peers, 2 * slice_rows, width), BOTH, 0, 0...  3.21 us
  transfers between devices with their start and end apart: 4, of which 4 were waited for; matrix products, arithmetic and copies ran while one was open for 6% of the time, Pallas kernels for 10%

profile of v5, /device:TPU:6, one launch (start us, length us, event | category | flops | bytes accessed | tf_op | source)
XLA Modules:
  0.0 58.3 jit_solution(6660948416794000816)
XLA Ops:
  0.6 3.7 %collective-permute-start = (bf16[8,1024]{1,0:T(8,128)(2,1)}, bf16[8,1024]{1,0:T(8,128)(2,1)S(1)}, u32[]{:S(2)}, u32[]{:S(2)}) collective-permute-start(bf16[8,1024]{1,0:T(8,128)(2,1)} %param.9), channel_id=1, source_target_pairs={{0,24},{8,16},{16,40},{24,32},{32,56},{40,48},{48,72},{56,64},{64,... | collective-permute-start | bytes 49160 | tf_op jit(solution)/shard_map/ppermute | solution.py:133
  4.4 1.6 %broadcast_in_dim.8 = bf16[16,2,8,1024]{3,2,1,0:T(8,128)(2,1)} broadcast(bf16[8,1024]{1,0:T(8,128)(2,1)} %param.9), dimensions={2,3} | broadcast | bytes 540672 | tf_op jit(solution)/shard_map/broadcast_in_dim | solution.py:131
  6.0 11.6 %collective-permute-done = bf16[8,1024]{1,0:T(8,128)(2,1)S(1)} collective-permute-done((bf16[8,1024]{1,0:T(8,128)(2,1)}, bf16[8,1024]{1,0:T(8,128)(2,1)S(1)}, u32[]{:S(2)}, u32[]{:S(2)}) %collective-permute-start) | collective-permute-done | bytes 16416 | tf_op jit(solution)/shard_map/ppermute | solution.py:133
  17.6 0.7 %broadcast_dynamic-update-slice_fusion = bf16[16,2,8,1024]{3,2,1,0:T(8,128)(2,1)} fusion(bf16[16,2,8,1024]{3,2,1,0:T(8,128)(2,1)} %broadcast_in_dim.8, bf16[8,1024]{1,0:T(8,128)(2,1)S(1)} %collective-permute-done), kind=kLoop, calls=%fused_computation | loop fusion | bytes 278528 | tf_op jit(solution)/shard_map/dynamic_update_slice | solution.py:135
  18.3 3.5 %all-to-all-start = ((bf16[16,16,1024]{2,1,0:T(8,128)(2,1)}), bf16[16,16,1024]{2,1,0:T(8,128)(2,1)S(1)}, u32[]{:S(2)}, u32[]{:S(2)}) async-start(bf16[16,16,1024]{2,1,0:T(8,128)(2,1)} %bitcast.1), calls=%async_computation | async-start | bytes 1048576 | tf_op jit(solution)/shard_map/all_to_all | solution.py:136
  21.8 0.0 copy-start
  21.9 0.0 copy-start.1
  21.9 6.1 %shard_map.103 = (bf16[384,1024]{1,0:T(8,128)(2,1)S(1)}, bf16[384,1024]{1,0:T(8,128)(2,1)S(1)}, f32[4,96,96]{2,1,0:T(8,128)S(1)}) custom-call(bf16[384,1024]{1,0:T(8,128)(2,1)} %bitcast.19, bf16[1024,1024]{1,0:T(8,128)(2,1)} %key_hbm.1, bf16[1024,1024]{1,0:T(8,128)(2,1)} %query_hbm.1, bf16[1024,1024]{1,0:T(8,128)(2,1)} %value_hbm.1, bf16[1024,1024]{1,0:T(8,128)(2,1)} %out_hbm.1), custom_call_target="tpu_custom_call" | custom-call | flops 3221225472 | bytes 8388608 | tf_op jit(solution)/shard_map/pallas_call | solution.py:144
  27.9 3.2 %all-to-all-done = bf16[16,16,1024]{2,1,0:T(8,128)(2,1)S(1)} async-done(((bf16[16,16,1024]{2,1,0:T(8,128)(2,1)}), bf16[16,16,1024]{2,1,0:T(8,128)(2,1)S(1)}, u32[]{:S(2)}, u32[]{:S(2)}) %all-to-all-start) | async-done | bytes 524320 | tf_op jit(solution)/shard_map/all_to_all | solution.py:136
  31.1 0.0 copy-done
  31.1 0.0 copy-done.1
  31.1 1.7 %shard_map.104 = (f32[4,256]{1,0:T(4,128)S(1)}, f32[4,128]{1,0:T(4,128)S(1)}, f32[1,256]{1,0:T(1,128)S(1)}) custom-call(s32[1]{0:T(128)} %bitcast.place_ref, s32[4]{0:T(128)S(1)} %copy-done, s32[4]{0:T(128)S(1)} %copy-done.1, bf16[256,1024]{1,0:T(8,128)(2,1)S(1)} %bitcast.16, bf16[384,1024]{1,0:T(8,128)(2,1)S(1)} %get-tuple-element.9.key_ref, ...), custom_call_target="tpu_custom_call" | custom-call | flops 500000000 | bytes 3000000 | tf_op jit(solution)/shard_map/pallas_call | solution.py:165
  32.8 0.6 %broadcast_in_dim.11 = f32[32,1,256]{2,1,0:T(1,128)} broadcast(f32[256]{0:T(256)S(1)} %bitcast.17), dimensions={2} | broadcast | bytes 33792 | tf_op jit(solution)/shard_map/broadcast_in_dim | solution.py:179
  33.4 12.6 %all-to-all-start.1 = ((f32[32,1,256]{2,1,0:T(1,128)}), f32[32,1,256]{2,1,0:T(1,128)S(1)}, u32[]{:S(2)}, u32[]{:S(2)}) async-start(f32[32,1,256]{2,1,0:T(1,128)} %broadcast_in_dim.11), calls=%async_computation.1 | async-start | bytes 65536 | tf_op jit(solution)/shard_map/all_to_all | solution.py:180
  46.1 0.1 reshape.96
  46.2 0.2 fusion
  46.4 0.1 select_n.90
  46.5 0.1 select_n.92
  46.5 0.1 select_n.94
  46.6 0.6 %pad_maximum_fusion = f32[4,3,64]{2,0,1:T(4,128)} fusion(f32[4,1,64]{2,0,1:T(4,128)S(1)} %select_n.94, f32[4,1,64]{2,0,1:T(4,128)S(1)} %select_n.92, f32[4,1,64]{2,0,1:T(4,128)S(1)} %select_n.90), kind=kLoop, calls=%fused_computation.7 | loop fusion | flops 1536 | bytes 6144 | tf_op jit(solution)/shard_map/stack | solution.py:205
  47.2 0.6 %slice_reduce_fusion = f32[4]{0:T(128)} fusion(f32[4,128]{1,0:T(4,128)S(1)} %get-tuple-element.13), kind=kLoop, calls=%fused_computation.8 | loop fusion | bytes 32 | tf_op jit(solution)/shard_map/slice | solution.py:205
  47.8 3.7 %all-to-all-done.1 = f32[32,1,256]{2,1,0:T(1,128)S(1)} async-done(((f32[32,1,256]{2,1,0:T(1,128)}), f32[32,1,256]{2,1,0:T(1,128)S(1)}, u32[]{:S(2)}, u32[]{:S(2)}) %all-to-all-start.1) | async-done | bytes 32800 | tf_op jit(solution)/shard_map/all_to_all | solution.py:180
  51.6 0.1 constant_dynamic-slice_fusion.1
  51.7 4.9 %collective-permute-start.1 = (f32[8]{0:T(128)S(1)}, f32[8]{0:T(128)S(1)}, u32[]{:S(2)}, u32[]{:S(2)}) collective-permute-start(f32[8]{0:T(128)S(1)} %fusion.6), channel_id=1, source_target_pairs={{16,1008},{24,1016},{48,16},{56,24},{80,48},{88,56},{112,80},{120,... | collective-permute-start | bytes 104 | tf_op jit(solution)/shard_map/ppermute | solution.py:28
  56.5 1.3 %collective-permute-done.1 = f32[8]{0:T(128)S(1)} collective-permute-done((f32[8]{0:T(128)S(1)}, f32[8]{0:T(128)S(1)}, u32[]{:S(2)}, u32[]{:S(2)}) %collective-permute-start.1) | collective-permute-done | bytes 64 | tf_op jit(solution)/shard_map/ppermute | solution.py:28
  57.8 0.5 fusion.5
  (3 shorter events, 0.0 us)
Async XLA Ops:
  0.6 17.0 %collective-permute-start = (bf16[8,1024]{1,0:T(8,128)(2,1)}, bf16[8,1024]{1,0:T(8,128)(2,1)S(1)}, u32[]{:S(2)}, u32[]{:S(2)}) collective-permute-start(bf16[8,1024]{1,0:T(8,128)(2,1)} %param.9), channel_id=1, source_target_pairs={{0,24},{8,16},{16,40},{24,32},{32,56},{40,48},{48,72},{56,64},{64,... | collective-permute-start | bytes 49160 | tf_op jit(solution)/shard_map/ppermute | solution.py:133
  18.3 12.8 %all-to-all-start = ((bf16[16,16,1024]{2,1,0:T(8,128)(2,1)}), bf16[16,16,1024]{2,1,0:T(8,128)(2,1)S(1)}, u32[]{:S(2)}, u32[]{:S(2)}) async-start(bf16[16,16,1024]{2,1,0:T(8,128)(2,1)} %bitcast.1), calls=%async_computation | async-start | bytes 1048576 | tf_op jit(solution)/shard_map/all_to_all | solution.py:136
  21.8 9.3 %copy-start = (s32[4]{0:T(128)S(1)}, s32[4]{0:T(128)}, u32[]{:S(2)}) copy-start(s32[4]{0:T(128)} %counts_ref.1) | copy-start | bytes 52
  21.9 9.3 %copy-start.1 = (s32[4]{0:T(128)S(1)}, s32[4]{0:T(128)}, u32[]{:S(2)}) copy-start(s32[4]{0:T(128)} %pos_ref.1) | copy-start | bytes 52
  33.4 18.1 %all-to-all-start.1 = ((f32[32,1,256]{2,1,0:T(1,128)}), f32[32,1,256]{2,1,0:T(1,128)S(1)}, u32[]{:S(2)}, u32[]{:S(2)}) async-start(f32[32,1,256]{2,1,0:T(1,128)} %broadcast_in_dim.11), calls=%async_computation.1 | async-start | bytes 65536 | tf_op jit(solution)/shard_map/all_to_all | solution.py:180
  51.7 6.1 %collective-permute-start.1 = (f32[8]{0:T(128)S(1)}, f32[8]{0:T(128)S(1)}, u32[]{:S(2)}, u32[]{:S(2)}) collective-permute-start(f32[8]{0:T(128)S(1)} %fusion.6), channel_id=1, source_target_pairs={{16,1008},{24,1016},{48,16},{56,24},{80,48},{88,56},{112,80},{120,... | collective-permute-start | bytes 104 | tf_op jit(solution)/shard_map/ppermute | solution.py:28

commit v6 on v5

--- a/solution.py
+++ b/solution.py
@@ -110,7 +110,7 @@
     hop = place + jnp.where(older == 1, bringer + 1, -bringer)
     in_block = lane // (2 * SLICE) * SLICE % block + lane % SLICE
     exp_sims = jnp.where((hop >= 0) & (hop <= HOPS), jnp.exp(similar), 0.0)
-    terms_ref[...] = jnp.sum(exp_sims, axis=0, keepdims=True)
+    terms_ref[...] = jnp.broadcast_to(jnp.sum(exp_sims, axis=0, keepdims=True)[None], terms_ref.shape)
     similar_ref[...] = similar
     hit = (hop >= 0) & (hop <= HOPS) & (hop * block + in_block == position)
     picked = jnp.sum(jnp.where(hit, similar, 0.0), axis=1, keepdims=True)
@@ -169,16 +169,15 @@
         out_shape=[
             jax.ShapeDtypeStruct((clips, 2 * peers * slice_rows), F32),
             jax.ShapeDtypeStruct((clips, 128), F32),
-            jax.ShapeDtypeStruct((1, 2 * peers * slice_rows), F32),
+            jax.ShapeDtypeStruct((RING * tm_count, 1, 2 * peers * slice_rows), F32),
         ],
         compiler_params=pltpu.CompilerParams(vmem_limit_bytes=24 * 1024 * 1024),
         cost_estimate=pl.CostEstimate(flops=500_000_000, bytes_accessed=3_000_000, transcendentals=120_000),
     )(place.reshape(1), frame_counts, clip_pos, band_text, key_rows, value_rows, gram)
 
     similar, loss, terms = lax.optimization_barrier((similar, loss, terms))
-    met = jnp.broadcast_to(terms[None], (RING * tm_count,) + terms.shape)
     met = lax.all_to_all(
-        met, BOTH, 0, 0, axis_index_groups=block_groups(dp_count, tm_count, RING), tiled=True
+        terms, BOTH, 0, 0, axis_index_groups=block_groups(dp_count, tm_count, RING), tiled=True
     )
     met = jnp.sum(met.reshape(RING // PAIR, peers, -1), axis=1)
     mine = lax.axis_index("tm") * 2 * slice_rows

time: 58.7 us -> 58.6 us (level)
  local copies, waits for them, and re-layouts: 4.05 us -> 3.42 us
    broadcast_in_dim x1 -> x0, local copies, waits for them, and re-layouts: 0.63 us -> none  [local(): met = jnp.broadcast_to(terms[None], (RING * tm_count,) + terms.shape)]
where the time goes in v6:
time: 58.6 us; the launch traced here: 58.2 us
  starting transfers between devices  24.7 us (42%)
  waiting for transfers between devices  19.8 us (34%)
  Pallas kernels  8.28 us (14%)
  local copies, waits for them, and re-layouts  3.42 us (6%)
  other arithmetic  1.31 us (2%)
  between operations  0.75 us (1%)
    all_to_all x1, starting transfers between devices, local(): lax.all_to_all(terms, BOTH, 0, 0, axis_index_groups=block_groups(dp_count...  12.6 us
    ppermute x1, waiting for transfers between devices, local(): before = lax.ppermute(texts, 'dp', crossed)  11.6 us
    pallas_call x1, Pallas kernels, local(): pl.pallas_call(project_kernel, in_specs=[pl.BlockSpec(memory_space=pltpu....  6.06 us
    ppermute x1, starting transfers between devices, moved(): return lax.ppermute(value, 'dp', pairs)  4.86 us
    ppermute x1, starting transfers between devices, local(): before = lax.ppermute(texts, 'dp', crossed)  3.74 us
    all_to_all x1, waiting for transfers between devices, local(): lax.all_to_all(terms, BOTH, 0, 0, axis_index_groups=block_groups(dp_count...  3.7 us
    all_to_all x1, starting transfers between devices, local(): lax.all_to_all(outgoing.reshape(peers, 2 * slice_rows, width), BOTH, 0, 0...  3.47 us
    all_to_all x1, waiting for transfers between devices, local(): lax.all_to_all(outgoing.reshape(peers, 2 * slice_rows, width), BOTH, 0, 0...  3.21 us
  transfers between devices with their start and end apart: 4, of which 4 were waited for; matrix products, arithmetic and copies ran while one was open for 6% of the time, Pallas kernels for 10%

profile of v6, /device:TPU:6, one launch (start us, length us, event | category | flops | bytes accessed | tf_op | source)
XLA Modules:
  0.0 58.2 jit_solution(9498700245935815770)
XLA Ops:
  0.6 3.7 %collective-permute-start = (bf16[8,1024]{1,0:T(8,128)(2,1)}, bf16[8,1024]{1,0:T(8,128)(2,1)S(1)}, u32[]{:S(2)}, u32[]{:S(2)}) collective-permute-start(bf16[8,1024]{1,0:T(8,128)(2,1)} %param.9), channel_id=1, source_target_pairs={{0,24},{8,16},{16,40},{24,32},{32,56},{40,48},{48,72},{56,64},{64,... | collective-permute-start | bytes 49160 | tf_op jit(solution)/shard_map/ppermute | solution.py:133
  4.4 1.6 %broadcast_in_dim.4 = bf16[16,2,8,1024]{3,2,1,0:T(8,128)(2,1)} broadcast(bf16[8,1024]{1,0:T(8,128)(2,1)} %param.9), dimensions={2,3} | broadcast | bytes 540672 | tf_op jit(solution)/shard_map/broadcast_in_dim | solution.py:131
  6.0 11.6 %collective-permute-done = bf16[8,1024]{1,0:T(8,128)(2,1)S(1)} collective-permute-done((bf16[8,1024]{1,0:T(8,128)(2,1)}, bf16[8,1024]{1,0:T(8,128)(2,1)S(1)}, u32[]{:S(2)}, u32[]{:S(2)}) %collective-permute-start) | collective-permute-done | bytes 16416 | tf_op jit(solution)/shard_map/ppermute | solution.py:133
  17.6 0.7 %broadcast_dynamic-update-slice_fusion = bf16[16,2,8,1024]{3,2,1,0:T(8,128)(2,1)} fusion(bf16[16,2,8,1024]{3,2,1,0:T(8,128)(2,1)} %broadcast_in_dim.4, bf16[8,1024]{1,0:T(8,128)(2,1)S(1)} %collective-permute-done), kind=kLoop, calls=%fused_computation | loop fusion | bytes 278528 | tf_op jit(solution)/shard_map/dynamic_update_slice | solution.py:135
  18.3 3.5 %all-to-all-start = ((bf16[16,16,1024]{2,1,0:T(8,128)(2,1)}), bf16[16,16,1024]{2,1,0:T(8,128)(2,1)S(1)}, u32[]{:S(2)}, u32[]{:S(2)}) async-start(bf16[16,16,1024]{2,1,0:T(8,128)(2,1)} %bitcast.1), calls=%async_computation | async-start | bytes 1048576 | tf_op jit(solution)/shard_map/all_to_all | solution.py:136
  21.8 0.0 copy-start
  21.9 0.0 copy-start.1
  21.9 6.1 %shard_map.103 = (bf16[384,1024]{1,0:T(8,128)(2,1)S(1)}, bf16[384,1024]{1,0:T(8,128)(2,1)S(1)}, f32[4,96,96]{2,1,0:T(8,128)S(1)}) custom-call(bf16[384,1024]{1,0:T(8,128)(2,1)} %bitcast.17, bf16[1024,1024]{1,0:T(8,128)(2,1)} %key_hbm.1, bf16[1024,1024]{1,0:T(8,128)(2,1)} %query_hbm.1, bf16[1024,1024]{1,0:T(8,128)(2,1)} %value_hbm.1, bf16[1024,1024]{1,0:T(8,128)(2,1)} %out_hbm.1), custom_call_target="tpu_custom_call" | custom-call | flops 3221225472 | bytes 8388608 | tf_op jit(solution)/shard_map/pallas_call | solution.py:144
  27.9 3.2 %all-to-all-done = bf16[16,16,1024]{2,1,0:T(8,128)(2,1)S(1)} async-done(((bf16[16,16,1024]{2,1,0:T(8,128)(2,1)}), bf16[16,16,1024]{2,1,0:T(8,128)(2,1)S(1)}, u32[]{:S(2)}, u32[]{:S(2)}) %all-to-all-start) | async-done | bytes 524320 | tf_op jit(solution)/shard_map/all_to_all | solution.py:136
  31.1 0.0 copy-done
  31.1 0.0 copy-done.1
  31.1 2.2 %shard_map.104 = (f32[4,256]{1,0:T(4,128)S(1)}, f32[4,128]{1,0:T(4,128)S(1)}, f32[32,1,256]{2,1,0:T(1,128)}) custom-call(s32[1]{0:T(128)} %bitcast.place_ref, s32[4]{0:T(128)S(1)} %copy-done, s32[4]{0:T(128)S(1)} %copy-done.1, bf16[256,1024]{1,0:T(8,128)(2,1)S(1)} %bitcast.15, bf16[384,1024]{1,0:T(8,128)(2,1)S(1)} %get-tuple-element.9.key_ref, ...), custom_call_target="tpu_custom_call" | custom-call | flops 500000000 | bytes 3000000 | tf_op jit(solution)/shard_map/pallas_call | solution.py:165
  33.4 12.6 %all-to-all-start.1 = ((f32[32,1,256]{2,1,0:T(1,128)}), f32[32,1,256]{2,1,0:T(1,128)S(1)}, u32[]{:S(2)}, u32[]{:S(2)}) async-start(f32[32,1,256]{2,1,0:T(1,128)} %get-tuple-element.14), calls=%async_computation.1 | async-start | bytes 65536 | tf_op jit(solution)/shard_map/all_to_all | solution.py:179
  46.0 0.1 reshape.93
  46.1 0.2 fusion
  46.3 0.1 select_n.90
  46.4 0.1 select_n.92
  46.5 0.1 select_n.94
  46.5 0.6 %pad_maximum_fusion = f32[4,3,64]{2,0,1:T(4,128)} fusion(f32[4,1,64]{2,0,1:T(4,128)S(1)} %select_n.94, f32[4,1,64]{2,0,1:T(4,128)S(1)} %select_n.92, f32[4,1,64]{2,0,1:T(4,128)S(1)} %select_n.90), kind=kLoop, calls=%fused_computation.7 | loop fusion | flops 1536 | bytes 6144 | tf_op jit(solution)/shard_map/stack | solution.py:204
  47.1 0.6 %slice_reduce_fusion = f32[4]{0:T(128)} fusion(f32[4,128]{1,0:T(4,128)S(1)} %get-tuple-element.13), kind=kLoop, calls=%fused_computation.8 | loop fusion | bytes 32 | tf_op jit(solution)/shard_map/slice | solution.py:204
  47.8 3.7 %all-to-all-done.1 = f32[32,1,256]{2,1,0:T(1,128)S(1)} async-done(((f32[32,1,256]{2,1,0:T(1,128)}), f32[32,1,256]{2,1,0:T(1,128)S(1)}, u32[]{:S(2)}, u32[]{:S(2)}) %all-to-all-start.1) | async-done | bytes 32800 | tf_op jit(solution)/shard_map/all_to_all | solution.py:179
  51.5 0.1 constant_dynamic-slice_fusion.1
  51.6 4.9 %collective-permute-start.1 = (f32[8]{0:T(128)S(1)}, f32[8]{0:T(128)S(1)}, u32[]{:S(2)}, u32[]{:S(2)}) collective-permute-start(f32[8]{0:T(128)S(1)} %fusion.6), channel_id=1, source_target_pairs={{16,1008},{24,1016},{48,16},{56,24},{80,48},{88,56},{112,80},{120,... | collective-permute-start | bytes 104 | tf_op jit(solution)/shard_map/ppermute | solution.py:28
  56.4 1.3 %collective-permute-done.1 = f32[8]{0:T(128)S(1)} collective-permute-done((f32[8]{0:T(128)S(1)}, f32[8]{0:T(128)S(1)}, u32[]{:S(2)}, u32[]{:S(2)}) %collective-permute-start.1) | collective-permute-done | bytes 64 | tf_op jit(solution)/shard_map/ppermute | solution.py:28
  57.7 0.5 fusion.5
  (3 shorter events, 0.0 us)
Async XLA Ops:
  0.6 17.0 %collective-permute-start = (bf16[8,1024]{1,0:T(8,128)(2,1)}, bf16[8,1024]{1,0:T(8,128)(2,1)S(1)}, u32[]{:S(2)}, u32[]{:S(2)}) collective-permute-start(bf16[8,1024]{1,0:T(8,128)(2,1)} %param.9), channel_id=1, source_target_pairs={{0,24},{8,16},{16,40},{24,32},{32,56},{40,48},{48,72},{56,64},{64,... | collective-permute-start | bytes 49160 | tf_op jit(solution)/shard_map/ppermute | solution.py:133
  18.3 12.8 %all-to-all-start = ((bf16[16,16,1024]{2,1,0:T(8,128)(2,1)}), bf16[16,16,1024]{2,1,0:T(8,128)(2,1)S(1)}, u32[]{:S(2)}, u32[]{:S(2)}) async-start(bf16[16,16,1024]{2,1,0:T(8,128)(2,1)} %bitcast.1), calls=%async_computation | async-start | bytes 1048576 | tf_op jit(solution)/shard_map/all_to_all | solution.py:136
  21.8 9.3 %copy-start = (s32[4]{0:T(128)S(1)}, s32[4]{0:T(128)}, u32[]{:S(2)}) copy-start(s32[4]{0:T(128)} %counts_ref.1) | copy-start | bytes 52
  21.9 9.3 %copy-start.1 = (s32[4]{0:T(128)S(1)}, s32[4]{0:T(128)}, u32[]{:S(2)}) copy-start(s32[4]{0:T(128)} %pos_ref.1) | copy-start | bytes 52
  33.4 18.1 %all-to-all-start.1 = ((f32[32,1,256]{2,1,0:T(1,128)}), f32[32,1,256]{2,1,0:T(1,128)S(1)}, u32[]{:S(2)}, u32[]{:S(2)}) async-start(f32[32,1,256]{2,1,0:T(1,128)} %get-tuple-element.14), calls=%async_computation.1 | async-start | bytes 65536 | tf_op jit(solution)/shard_map/all_to_all | solution.py:179
  51.6 6.1 %collective-permute-start.1 = (f32[8]{0:T(128)S(1)}, f32[8]{0:T(128)S(1)}, u32[]{:S(2)}, u32[]{:S(2)}) collective-permute-start(f32[8]{0:T(128)S(1)} %fusion.6), channel_id=1, source_target_pairs={{16,1008},{24,1016},{48,16},{56,24},{80,48},{88,56},{112,80},{120,... | collective-permute-start | bytes 104 | tf_op jit(solution)/shard_map/ppermute | solution.py:28

commit v7 on v6

--- a/solution.py
+++ b/solution.py
@@ -175,7 +175,6 @@
         cost_estimate=pl.CostEstimate(flops=500_000_000, bytes_accessed=3_000_000, transcendentals=120_000),
     )(place.reshape(1), frame_counts, clip_pos, band_text, key_rows, value_rows, gram)
 
-    similar, loss, terms = lax.optimization_barrier((similar, loss, terms))
     met = lax.all_to_all(
         terms, BOTH, 0, 0, axis_index_groups=block_groups(dp_count, tm_count, RING), tiled=True
     )
@@ -187,6 +186,7 @@
     later = lax.axis_index("dp") % RING >= PAIR
     newer = jnp.where(later, newer[1], newer[0])
     older = jnp.where(later, older[0], older[1])
+    similar, loss, older = lax.optimization_barrier((similar, loss, older))
     beyond = moved(older, -RING, range(PAIR, RING))
     text_lse = jnp.log(newer + jnp.where(later, beyond, older))
 

time: 58.6 us -> 59.2 us (1.010)
  waiting for transfers between devices: 19.8 us -> 20.4 us
    all_to_all x1, waiting for transfers between devices: 3.7 us -> 5.45 us  [local(): lax.all_to_all(terms, BOTH, 0, 0, axis_index_groups=block_groups(dp_count...]
    ppermute x1, waiting for transfers between devices: 1.27 us -> 0.11 us  [moved(): return lax.ppermute(value, 'dp', pairs)]
  transfers between devices with their start and end apart: 4 -> 4, of which waited for: 4 -> 4; matrix products, arithmetic and copies ran while one was open for 6% -> 5% of each run, Pallas kernels for 10% -> 10%
where the time goes in v7:
time: 59.2 us; the launch traced here: 58.9 us
  starting transfers between devices  24.7 us (42%)
  waiting for transfers between devices  20.4 us (34%)
  Pallas kernels  8.27 us (14%)
  local copies, waits for them, and re-layouts  3.42 us (6%)
  other arithmetic  1.31 us (2%)
  between operations  0.76 us (1%)
    all_to_all x1, starting transfers between devices, local(): lax.all_to_all(terms, BOTH, 0, 0, axis_index_groups=block_groups(dp_count...  12.6 us
    ppermute x1, waiting for transfers between devices, local(): before = lax.ppermute(texts, 'dp', crossed)  11.6 us
    pallas_call x1, Pallas kernels, local(): pl.pallas_call(project_kernel, in_specs=[pl.BlockSpec(memory_space=pltpu....  6.05 us
    all_to_all x1, waiting for transfers between devices, local(): lax.all_to_all(terms, BOTH, 0, 0, axis_index_groups=block_groups(dp_count...  5.45 us
    ppermute x1, starting transfers between devices, moved(): return lax.ppermute(value, 'dp', pairs)  4.86 us
    ppermute x1, starting transfers between devices, local(): before = lax.ppermute(texts, 'dp', crossed)  3.74 us
    all_to_all x1, starting transfers between devices, local(): lax.all_to_all(outgoing.reshape(peers, 2 * slice_rows, width), BOTH, 0, 0...  3.47 us
    all_to_all x1, waiting for transfers between devices, local(): lax.all_to_all(outgoing.reshape(peers, 2 * slice_rows, width), BOTH, 0, 0...  3.24 us
  transfers between devices with their start and end apart: 4, of which 4 were waited for; matrix products, arithmetic and copies ran while one was open for 5% of the time, Pallas kernels for 10%

profile of v7, /device:TPU:6, one launch (start us, length us, event | category | flops | bytes accessed | tf_op | source)
XLA Modules:
  0.0 58.9 jit_solution(15592473141083924216)
XLA Ops:
  0.6 3.7 %collective-permute-start = (bf16[8,1024]{1,0:T(8,128)(2,1)}, bf16[8,1024]{1,0:T(8,128)(2,1)S(1)}, u32[]{:S(2)}, u32[]{:S(2)}) collective-permute-start(bf16[8,1024]{1,0:T(8,128)(2,1)} %param.9), channel_id=1, source_target_pairs={{0,24},{8,16},{16,40},{24,32},{32,56},{40,48},{48,72},{56,64},{64,... | collective-permute-start | bytes 49160 | tf_op jit(solution)/shard_map/ppermute | solution.py:133
  4.4 1.6 %broadcast_in_dim.4 = bf16[16,2,8,1024]{3,2,1,0:T(8,128)(2,1)} broadcast(bf16[8,1024]{1,0:T(8,128)(2,1)} %param.9), dimensions={2,3} | broadcast | bytes 540672 | tf_op jit(solution)/shard_map/broadcast_in_dim | solution.py:131
  6.0 11.6 %collective-permute-done = bf16[8,1024]{1,0:T(8,128)(2,1)S(1)} collective-permute-done((bf16[8,1024]{1,0:T(8,128)(2,1)}, bf16[8,1024]{1,0:T(8,128)(2,1)S(1)}, u32[]{:S(2)}, u32[]{:S(2)}) %collective-permute-start) | collective-permute-done | bytes 16416 | tf_op jit(solution)/shard_map/ppermute | solution.py:133
  17.6 0.7 %broadcast_dynamic-update-slice_fusion = bf16[16,2,8,1024]{3,2,1,0:T(8,128)(2,1)} fusion(bf16[16,2,8,1024]{3,2,1,0:T(8,128)(2,1)} %broadcast_in_dim.4, bf16[8,1024]{1,0:T(8,128)(2,1)S(1)} %collective-permute-done), kind=kLoop, calls=%fused_computation | loop fusion | bytes 278528 | tf_op jit(solution)/shard_map/dynamic_update_slice | solution.py:135
  18.3 3.5 %all-to-all-start = ((bf16[16,16,1024]{2,1,0:T(8,128)(2,1)}), bf16[16,16,1024]{2,1,0:T(8,128)(2,1)S(1)}, u32[]{:S(2)}, u32[]{:S(2)}) async-start(bf16[16,16,1024]{2,1,0:T(8,128)(2,1)} %bitcast.1), calls=%async_computation | async-start | bytes 1048576 | tf_op jit(solution)/shard_map/all_to_all | solution.py:136
  21.8 0.0 copy-start
  21.8 0.0 copy-start.1
  21.8 6.1 %shard_map.103 = (bf16[384,1024]{1,0:T(8,128)(2,1)S(1)}, bf16[384,1024]{1,0:T(8,128)(2,1)S(1)}, f32[4,96,96]{2,1,0:T(8,128)S(1)}) custom-call(bf16[384,1024]{1,0:T(8,128)(2,1)} %bitcast.15, bf16[1024,1024]{1,0:T(8,128)(2,1)} %key_hbm.1, bf16[1024,1024]{1,0:T(8,128)(2,1)} %query_hbm.1, bf16[1024,1024]{1,0:T(8,128)(2,1)} %value_hbm.1, bf16[1024,1024]{1,0:T(8,128)(2,1)} %out_hbm.1), custom_call_target="tpu_custom_call" | custom-call | flops 3221225472 | bytes 8388608 | tf_op jit(solution)/shard_map/pallas_call | solution.py:144
  27.9 3.2 %all-to-all-done = bf16[16,16,1024]{2,1,0:T(8,128)(2,1)S(1)} async-done(((bf16[16,16,1024]{2,1,0:T(8,128)(2,1)}), bf16[16,16,1024]{2,1,0:T(8,128)(2,1)S(1)}, u32[]{:S(2)}, u32[]{:S(2)}) %all-to-all-start) | async-done | bytes 524320 | tf_op jit(solution)/shard_map/all_to_all | solution.py:136
  31.1 0.0 copy-done
  31.1 0.0 copy-done.1
  31.1 2.2 %shard_map.104 = (f32[4,256]{1,0:T(4,128)S(1)}, f32[4,128]{1,0:T(4,128)S(1)}, f32[32,1,256]{2,1,0:T(1,128)}) custom-call(s32[1]{0:T(128)} %bitcast.place_ref, s32[4]{0:T(128)S(1)} %copy-done, s32[4]{0:T(128)S(1)} %copy-done.1, bf16[256,1024]{1,0:T(8,128)(2,1)S(1)} %bitcast.13, bf16[384,1024]{1,0:T(8,128)(2,1)S(1)} %get-tuple-element.12.key_ref, ...), custom_call_target="tpu_custom_call" | custom-call | flops 500000000 | bytes 3000000 | tf_op jit(solution)/shard_map/pallas_call | solution.py:165
  33.4 12.6 %all-to-all-start.1 = ((f32[32,1,256]{2,1,0:T(1,128)}), f32[32,1,256]{2,1,0:T(1,128)S(1)}, u32[]{:S(2)}, u32[]{:S(2)}) async-start(f32[32,1,256]{2,1,0:T(1,128)} %get-tuple-element.17), calls=%async_computation.1 | async-start | bytes 65536 | tf_op jit(solution)/shard_map/all_to_all | solution.py:178
  46.0 5.5 %all-to-all-done.1 = f32[32,1,256]{2,1,0:T(1,128)S(1)} async-done(((f32[32,1,256]{2,1,0:T(1,128)}), f32[32,1,256]{2,1,0:T(1,128)S(1)}, u32[]{:S(2)}, u32[]{:S(2)}) %all-to-all-start.1) | async-done | bytes 32800 | tf_op jit(solution)/shard_map/all_to_all | solution.py:178
  51.5 0.1 constant_dynamic-slice_fusion
  51.6 0.6 %slice_reduce_fusion = f32[4]{0:T(128)} fusion(f32[4,128]{1,0:T(4,128)S(1)} %get-tuple-element.19), kind=kLoop, calls=%fused_computation.8 | loop fusion | bytes 32 | tf_op jit(solution)/shard_map/slice | solution.py:204
  52.2 4.9 %collective-permute-start.1 = (f32[8]{0:T(128)S(1)}, f32[8]{0:T(128)S(1)}, u32[]{:S(2)}, u32[]{:S(2)}) collective-permute-start(f32[8]{0:T(128)S(1)} %fusion.3), channel_id=1, source_target_pairs={{16,1008},{24,1016},{48,16},{56,24},{80,48},{88,56},{112,80},{120,... | collective-permute-start | bytes 104 | tf_op jit(solution)/shard_map/ppermute | solution.py:28
  57.1 0.1 reshape.94
  57.2 0.2 fusion
  57.4 0.1 select_n.95
  57.5 0.1 select_n.97
  57.5 0.1 select_n.99
  57.6 0.6 %pad_maximum_fusion = f32[4,3,64]{2,0,1:T(4,128)} fusion(f32[4,1,64]{2,0,1:T(4,128)S(1)} %select_n.99, f32[4,1,64]{2,0,1:T(4,128)S(1)} %select_n.97, f32[4,1,64]{2,0,1:T(4,128)S(1)} %select_n.95), kind=kLoop, calls=%fused_computation.7 | loop fusion | flops 1536 | bytes 6144 | tf_op jit(solution)/shard_map/stack | solution.py:204
  58.2 0.1 collective-permute-done.1
  58.3 0.5 fusion.6
  (3 shorter events, 0.0 us)
Async XLA Ops:
  0.6 17.0 %collective-permute-start = (bf16[8,1024]{1,0:T(8,128)(2,1)}, bf16[8,1024]{1,0:T(8,128)(2,1)S(1)}, u32[]{:S(2)}, u32[]{:S(2)}) collective-permute-start(bf16[8,1024]{1,0:T(8,128)(2,1)} %param.9), channel_id=1, source_target_pairs={{0,24},{8,16},{16,40},{24,32},{32,56},{40,48},{48,72},{56,64},{64,... | collective-permute-start | bytes 49160 | tf_op jit(solution)/shard_map/ppermute | solution.py:133
  18.3 12.8 %all-to-all-start = ((bf16[16,16,1024]{2,1,0:T(8,128)(2,1)}), bf16[16,16,1024]{2,1,0:T(8,128)(2,1)S(1)}, u32[]{:S(2)}, u32[]{:S(2)}) async-start(bf16[16,16,1024]{2,1,0:T(8,128)(2,1)} %bitcast.1), calls=%async_computation | async-start | bytes 1048576 | tf_op jit(solution)/shard_map/all_to_all | solution.py:136
  21.8 9.3 %copy-start = (s32[4]{0:T(128)S(1)}, s32[4]{0:T(128)}, u32[]{:S(2)}) copy-start(s32[4]{0:T(128)} %counts_ref.1) | copy-start | bytes 52
  21.8 9.3 %copy-start.1 = (s32[4]{0:T(128)S(1)}, s32[4]{0:T(128)}, u32[]{:S(2)}) copy-start(s32[4]{0:T(128)} %pos_ref.1) | copy-start | bytes 52
  33.4 18.1 %all-to-all-start.1 = ((f32[32,1,256]{2,1,0:T(1,128)}), f32[32,1,256]{2,1,0:T(1,128)S(1)}, u32[]{:S(2)}, u32[]{:S(2)}) async-start(f32[32,1,256]{2,1,0:T(1,128)} %get-tuple-element.17), calls=%async_computation.1 | async-start | bytes 65536 | tf_op jit(solution)/shard_map/all_to_all | solution.py:178
  52.2 6.1 %collective-permute-start.1 = (f32[8]{0:T(128)S(1)}, f32[8]{0:T(128)S(1)}, u32[]{:S(2)}, u32[]{:S(2)}) collective-permute-start(f32[8]{0:T(128)S(1)} %fusion.3), channel_id=1, source_target_pairs={{16,1008},{24,1016},{48,16},{56,24},{80,48},{88,56},{112,80},{120,... | collective-permute-start | bytes 104 | tf_op jit(solution)/shard_map/ppermute | solution.py:28

commit v8 on v6

--- a/solution.py
+++ b/solution.py
@@ -115,7 +115,10 @@
     hit = (hop >= 0) & (hop <= HOPS) & (hop * block + in_block == position)
     picked = jnp.sum(jnp.where(hit, similar, 0.0), axis=1, keepdims=True)
     total = jnp.sum(exp_sims, axis=1, keepdims=True)
-    loss_ref[...] = jnp.broadcast_to(jnp.log(total) - picked, loss_ref.shape)
+    loss = jnp.log(total) - picked
+    square = (clips, clips)
+    same = lax.broadcasted_iota(jnp.int32, square, 0) == lax.broadcasted_iota(jnp.int32, square, 1)
+    loss_ref[...] = jnp.sum(jnp.where(same, loss, 0.0), axis=0, keepdims=True)
 
 
 def local(frames, texts, w_query, w_key, w_value, w_out, frame_counts, clip_pos):
@@ -168,7 +171,7 @@
         out_specs=[vmem] * 3,
         out_shape=[
             jax.ShapeDtypeStruct((clips, 2 * peers * slice_rows), F32),
-            jax.ShapeDtypeStruct((clips, 128), F32),
+            jax.ShapeDtypeStruct((1, clips), F32),
             jax.ShapeDtypeStruct((RING * tm_count, 1, 2 * peers * slice_rows), F32),
         ],
         compiler_params=pltpu.CompilerParams(vmem_limit_bytes=24 * 1024 * 1024),
@@ -201,7 +204,7 @@
         jnp.where(first, part(0, 1), part(0, 0)),
         jnp.where(first, part(1, 1), part(0, 1)),
     ]
-    return (jnp.stack(by_hop, axis=1), loss[:, 0], text_lse)
+    return (jnp.stack(by_hop, axis=1), loss.reshape(clips), text_lse)
 
 
 def solution(mesh):

time: 58.6 us -> 58.6 us (level)
  local copies, waits for them, and re-layouts: 3.42 us -> 2.79 us
  waiting for transfers between devices: 19.8 us -> 20.4 us
    all_to_all x1, waiting for transfers between devices: 3.7 us -> 4.33 us  [local(): lax.all_to_all(terms, BOTH, 0, 0, axis_index_groups=block_groups(dp_count...]
    slice x1 -> x0, local copies, waits for them, and re-layouts: 0.63 us -> none  [local(): return (jnp.stack(by_hop, axis=1), loss[:, 0], text_lse)]
  transfers between devices with their start and end apart: 4 -> 4, of which waited for: 4 -> 4; matrix products, arithmetic and copies ran while one was open for 6% -> 5% of each run, Pallas kernels for 10% -> 10%
where the time goes in v8:
time: 58.6 us; the launch traced here: 58.3 us
  starting transfers between devices  24.7 us (42%)
  waiting for transfers between devices  20.4 us (35%)
  Pallas kernels  8.28 us (14%)
  local copies, waits for them, and re-layouts  2.79 us (5%)
  other arithmetic  1.31 us (2%)
  between operations  0.75 us (1%)
    all_to_all x1, starting transfers between devices, local(): lax.all_to_all(terms, BOTH, 0, 0, axis_index_groups=block_groups(dp_count...  12.6 us
    ppermute x1, waiting for transfers between devices, local(): before = lax.ppermute(texts, 'dp', crossed)  11.6 us
    pallas_call x1, Pallas kernels, local(): pl.pallas_call(project_kernel, in_specs=[pl.BlockSpec(memory_space=pltpu....  6.06 us
    ppermute x1, starting transfers between devices, moved(): return lax.ppermute(value, 'dp', pairs)  4.87 us
    all_to_all x1, waiting for transfers between devices, local(): lax.all_to_all(terms, BOTH, 0, 0, axis_index_groups=block_groups(dp_count...  4.33 us
    ppermute x1, starting transfers between devices, local(): before = lax.ppermute(texts, 'dp', crossed)  3.74 us
    all_to_all x1, starting transfers between devices, local(): lax.all_to_all(outgoing.reshape(peers, 2 * slice_rows, width), BOTH, 0, 0...  3.47 us
    all_to_all x1, waiting for transfers between devices, local(): lax.all_to_all(outgoing.reshape(peers, 2 * slice_rows, width), BOTH, 0, 0...  3.21 us
  transfers between devices with their start and end apart: 4, of which 4 were waited for; matrix products, arithmetic and copies ran while one was open for 5% of the time, Pallas kernels for 10%

profile of v8, /device:TPU:6, one launch (start us, length us, event | category | flops | bytes accessed | tf_op | source)
XLA Modules:
  0.0 58.3 jit_solution(11703154391999735626)
XLA Ops:
  0.6 3.7 %collective-permute-start = (bf16[8,1024]{1,0:T(8,128)(2,1)}, bf16[8,1024]{1,0:T(8,128)(2,1)S(1)}, u32[]{:S(2)}, u32[]{:S(2)}) collective-permute-start(bf16[8,1024]{1,0:T(8,128)(2,1)} %param.9), channel_id=1, source_target_pairs={{0,24},{8,16},{16,40},{24,32},{32,56},{40,48},{48,72},{56,64},{64,... | collective-permute-start | bytes 49160 | tf_op jit(solution)/shard_map/ppermute | solution.py:136
  4.4 1.6 %broadcast_in_dim.4 = bf16[16,2,8,1024]{3,2,1,0:T(8,128)(2,1)} broadcast(bf16[8,1024]{1,0:T(8,128)(2,1)} %param.9), dimensions={2,3} | broadcast | bytes 540672 | tf_op jit(solution)/shard_map/broadcast_in_dim | solution.py:134
  5.9 11.6 %collective-permute-done = bf16[8,1024]{1,0:T(8,128)(2,1)S(1)} collective-permute-done((bf16[8,1024]{1,0:T(8,128)(2,1)}, bf16[8,1024]{1,0:T(8,128)(2,1)S(1)}, u32[]{:S(2)}, u32[]{:S(2)}) %collective-permute-start) | collective-permute-done | bytes 16416 | tf_op jit(solution)/shard_map/ppermute | solution.py:136
  17.6 0.7 %broadcast_dynamic-update-slice_fusion = bf16[16,2,8,1024]{3,2,1,0:T(8,128)(2,1)} fusion(bf16[16,2,8,1024]{3,2,1,0:T(8,128)(2,1)} %broadcast_in_dim.4, bf16[8,1024]{1,0:T(8,128)(2,1)S(1)} %collective-permute-done), kind=kLoop, calls=%fused_computation | loop fusion | bytes 278528 | tf_op jit(solution)/shard_map/dynamic_update_slice | solution.py:138
  18.3 3.5 %all-to-all-start = ((bf16[16,16,1024]{2,1,0:T(8,128)(2,1)}), bf16[16,16,1024]{2,1,0:T(8,128)(2,1)S(1)}, u32[]{:S(2)}, u32[]{:S(2)}) async-start(bf16[16,16,1024]{2,1,0:T(8,128)(2,1)} %bitcast.1), calls=%async_computation | async-start | bytes 1048576 | tf_op jit(solution)/shard_map/all_to_all | solution.py:139
  21.8 0.0 copy-start
  21.9 0.0 copy-start.1
  21.9 6.1 %shard_map.103 = (bf16[384,1024]{1,0:T(8,128)(2,1)S(1)}, bf16[384,1024]{1,0:T(8,128)(2,1)S(1)}, f32[4,96,96]{2,1,0:T(8,128)S(1)}) custom-call(bf16[384,1024]{1,0:T(8,128)(2,1)} %bitcast.18, bf16[1024,1024]{1,0:T(8,128)(2,1)} %key_hbm.1, bf16[1024,1024]{1,0:T(8,128)(2,1)} %query_hbm.1, bf16[1024,1024]{1,0:T(8,128)(2,1)} %value_hbm.1, bf16[1024,1024]{1,0:T(8,128)(2,1)} %out_hbm.1), custom_call_target="tpu_custom_call" | custom-call | flops 3221225472 | bytes 8388608 | tf_op jit(solution)/shard_map/pallas_call | solution.py:147
  27.9 3.2 %all-to-all-done = bf16[16,16,1024]{2,1,0:T(8,128)(2,1)S(1)} async-done(((bf16[16,16,1024]{2,1,0:T(8,128)(2,1)}), bf16[16,16,1024]{2,1,0:T(8,128)(2,1)S(1)}, u32[]{:S(2)}, u32[]{:S(2)}) %all-to-all-start) | async-done | bytes 524320 | tf_op jit(solution)/shard_map/all_to_all | solution.py:139
  31.1 0.0 copy-done
  31.1 0.0 copy-done.1
  31.1 2.2 %shard_map.104 = (f32[4,256]{1,0:T(4,128)S(1)}, f32[1,4]{1,0:T(1,128)}, f32[32,1,256]{2,1,0:T(1,128)}) custom-call(s32[1]{0:T(128)} %bitcast.place_ref, s32[4]{0:T(128)S(1)} %copy-done, s32[4]{0:T(128)S(1)} %copy-done.1, bf16[256,1024]{1,0:T(8,128)(2,1)S(1)} %bitcast.16, bf16[384,1024]{1,0:T(8,128)(2,1)S(1)} %get-tuple-element.9.key_ref, ...), custom_call_target="tpu_custom_call" | custom-call | flops 500000000 | bytes 3000000 | tf_op jit(solution)/shard_map/pallas_call | solution.py:168
  33.4 12.6 %all-to-all-start.1 = ((f32[32,1,256]{2,1,0:T(1,128)}), f32[32,1,256]{2,1,0:T(1,128)S(1)}, u32[]{:S(2)}, u32[]{:S(2)}) async-start(f32[32,1,256]{2,1,0:T(1,128)} %get-tuple-element.14), calls=%async_computation.1 | async-start | bytes 65536 | tf_op jit(solution)/shard_map/all_to_all | solution.py:182
  46.0 0.1 reshape.96
  46.1 0.2 fusion
  46.3 0.1 select_n.90
  46.4 0.1 select_n.92
  46.5 0.1 select_n.94
  46.5 0.6 %pad_maximum_fusion = f32[4,3,64]{2,0,1:T(4,128)} fusion(f32[4,1,64]{2,0,1:T(4,128)S(1)} %select_n.94, f32[4,1,64]{2,0,1:T(4,128)S(1)} %select_n.92, f32[4,1,64]{2,0,1:T(4,128)S(1)} %select_n.90), kind=kLoop, calls=%fused_computation.7 | loop fusion | flops 1536 | bytes 6144 | tf_op jit(solution)/shard_map/stack | solution.py:207
  47.1 4.3 %all-to-all-done.1 = f32[32,1,256]{2,1,0:T(1,128)S(1)} async-done(((f32[32,1,256]{2,1,0:T(1,128)}), f32[32,1,256]{2,1,0:T(1,128)S(1)}, u32[]{:S(2)}, u32[]{:S(2)}) %all-to-all-start.1) | async-done | bytes 32800 | tf_op jit(solution)/shard_map/all_to_all | solution.py:182
  51.5 0.1 constant_dynamic-slice_fusion.1
  51.6 4.9 %collective-permute-start.1 = (f32[8]{0:T(128)S(1)}, f32[8]{0:T(128)S(1)}, u32[]{:S(2)}, u32[]{:S(2)}) collective-permute-start(f32[8]{0:T(128)S(1)} %fusion.6), channel_id=1, source_target_pairs={{16,1008},{24,1016},{48,16},{56,24},{80,48},{88,56},{112,80},{120,... | collective-permute-start | bytes 104 | tf_op jit(solution)/shard_map/ppermute | solution.py:28
  56.5 1.3 %collective-permute-done.1 = f32[8]{0:T(128)S(1)} collective-permute-done((f32[8]{0:T(128)S(1)}, f32[8]{0:T(128)S(1)}, u32[]{:S(2)}, u32[]{:S(2)}) %collective-permute-start.1) | collective-permute-done | bytes 64 | tf_op jit(solution)/shard_map/ppermute | solution.py:28
  57.7 0.5 fusion.5
  (3 shorter events, 0.0 us)
Async XLA Ops:
  0.6 17.0 %collective-permute-start = (bf16[8,1024]{1,0:T(8,128)(2,1)}, bf16[8,1024]{1,0:T(8,128)(2,1)S(1)}, u32[]{:S(2)}, u32[]{:S(2)}) collective-permute-start(bf16[8,1024]{1,0:T(8,128)(2,1)} %param.9), channel_id=1, source_target_pairs={{0,24},{8,16},{16,40},{24,32},{32,56},{40,48},{48,72},{56,64},{64,... | collective-permute-start | bytes 49160 | tf_op jit(solution)/shard_map/ppermute | solution.py:136
  18.3 12.8 %all-to-all-start = ((bf16[16,16,1024]{2,1,0:T(8,128)(2,1)}), bf16[16,16,1024]{2,1,0:T(8,128)(2,1)S(1)}, u32[]{:S(2)}, u32[]{:S(2)}) async-start(bf16[16,16,1024]{2,1,0:T(8,128)(2,1)} %bitcast.1), calls=%async_computation | async-start | bytes 1048576 | tf_op jit(solution)/shard_map/all_to_all | solution.py:139
  21.8 9.3 %copy-start = (s32[4]{0:T(128)S(1)}, s32[4]{0:T(128)}, u32[]{:S(2)}) copy-start(s32[4]{0:T(128)} %counts_ref.1) | copy-start | bytes 52
  21.9 9.3 %copy-start.1 = (s32[4]{0:T(128)S(1)}, s32[4]{0:T(128)}, u32[]{:S(2)}) copy-start(s32[4]{0:T(128)} %pos_ref.1) | copy-start | bytes 52
  33.4 18.1 %all-to-all-start.1 = ((f32[32,1,256]{2,1,0:T(1,128)}), f32[32,1,256]{2,1,0:T(1,128)S(1)}, u32[]{:S(2)}, u32[]{:S(2)}) async-start(f32[32,1,256]{2,1,0:T(1,128)} %get-tuple-element.14), calls=%async_computation.1 | async-start | bytes 65536 | tf_op jit(solution)/shard_map/all_to_all | solution.py:182
  51.6 6.2 %collective-permute-start.1 = (f32[8]{0:T(128)S(1)}, f32[8]{0:T(128)S(1)}, u32[]{:S(2)}, u32[]{:S(2)}) collective-permute-start(f32[8]{0:T(128)S(1)} %fusion.6), channel_id=1, source_target_pairs={{16,1008},{24,1016},{48,16},{56,24},{80,48},{88,56},{112,80},{120,... | collective-permute-start | bytes 104 | tf_op jit(solution)/shard_map/ppermute | solution.py:28
